TPU v7x, 512 devices: a whole 4x4x16 slice. The times are simulated.
512 devices in a mesh: subj: 32 (over z, core), var: 16 (over x, y).
Axes of the slice: x: 4, y: 4, z: 16, core: 2. Of those that a mesh axis runs over, the one named last changes fastest.
Arguments:
- traits: bfloat16 [65536, 256], P('subj', 'var'), may hold values from -6 to 6
- kin_tiles: bfloat16 [384, 256, 256], P('subj'), may hold values from -0.25 to 0.25
- kin_index: int32 [384, 2], P('subj'), may hold values from 0 to 255, as said below
- dosages: bfloat16 [65536, 12288], P('subj', 'var'), may hold values from 0 to 255, as said below
Outputs:
- scores: float32 [12288, 256], P(('var', 'subj'))
Inputs may be any that keep to these rules, and one draw needn't show every extreme that they name: `kin_index`: rows t * 12 to (t + 1) * 12 - 1 hold tiles whose row block lies in t * 8 to (t + 1) * 8 - 1; every row block has its diagonal tile; counts per row block are uneven; a pair may repeat. `dosages`: whole numbers.
All inputs are finite; a program needn't handle non-finite values.
Results may differ from a plain program's by a relative error of at most 0.009.
Values may be sent and summed in bfloat16 or wider, within the bound.
No kernel may reach another device: no remote copies, remote signals or barrier semaphores. Data moves between devices by JAX's collectives and lax.ppermute only.
A program may use at most 64 MiB of HBM per device.

v0:
```python
import jax
import jax.numpy as jnp
from jax import lax
from jax.sharding import PartitionSpec as P


def sent_to_all(x, axis):
    copies = jnp.broadcast_to(x, (lax.axis_size(axis), *x.shape))
    return lax.all_to_all(copies, axis, split_axis=0, concat_axis=0, tiled=True)


def laid_out(blocks, dim):
    blocks = jnp.moveaxis(blocks, 0, dim)
    dims = blocks.shape
    return blocks.reshape(*dims[:dim], dims[dim] * dims[dim + 1], *dims[dim + 2 :])


def gathered_copies(x, axis, dim):
    blocks = sent_to_all(x, axis)
    return laid_out(blocks, dim)


def cut_along(x, dim, devices):
    dims = x.shape
    blocks = x.reshape(*dims[:dim], devices, dims[dim] // devices, *dims[dim + 1 :])
    return jnp.moveaxis(blocks, dim, 0)


def sum_at_owner(x, axis, dim):
    blocks = cut_along(x, dim, lax.axis_size(axis))
    arrived = lax.all_to_all(blocks, axis, split_axis=0, concat_axis=0, tiled=True)
    return arrived.sum(axis=0)


def kinship_apply(field, kin_tiles, kin_index):
    rows_here = field.shape[0]
    block = kin_tiles.shape[1]
    width = field.shape[1]
    blocks_dev = rows_here // block
    gathered = lax.all_gather(field, "subj", axis=0, tiled=True)
    slabs = gathered.reshape(-1, block, width)[kin_index[:, 1]]
    prods = jnp.einsum("tij,tjk->tik", kin_tiles, slabs, preferred_element_type=jnp.float32)
    row_local = kin_index[:, 0] - lax.axis_index("subj") * blocks_dev
    onehot = (row_local[None, :] == jnp.arange(blocks_dev, dtype=jnp.int32)[:, None]).astype(
        jnp.float32
    )
    summed = jnp.einsum("bt,tik->bik", onehot, prods)
    return summed.reshape(rows_here, width)


def on_device(traits, kin_tiles, kin_index, dosages):
    first = kinship_apply(traits, kin_tiles, kin_index)
    first_sent = first.astype(jnp.bfloat16)
    second = kinship_apply(first_sent, kin_tiles, kin_index)
    base = traits.astype(jnp.float32)
    whitened = (0.6 * base + 0.5 * first + 0.3 * (2.0 * second - base)).astype(jnp.bfloat16)
    subjects = traits.shape[0] * lax.axis_size("subj")
    scale = 1.0 / (127.5 * jnp.sqrt(jnp.float32(subjects)))
    contract = (((0,), (0,)), ((), ()))
    wide = gathered_copies(whitened, "var", 1)
    partial_scores = lax.dot_general(dosages, wide, contract, preferred_element_type=jnp.float32)
    scores = sum_at_owner(partial_scores, "subj", 0)
    return scores * scale


def solution(mesh):
    in_specs = (P("subj", "var"), P("subj", None, None), P("subj", None), P("subj", "var"))
    out_specs = P(("var", "subj"), None)
    return jax.shard_map(
        on_device, mesh=mesh, in_specs=in_specs, out_specs=out_specs, check_vma=False
    )
```

profile of v0, /device:TPU:1, one launch (start us, length us, event | category | flops | bytes accessed | tf_op | source)
XLA Modules:
  0.0 261.5 jit_solution(4800661068077211716)
XLA Ops:
  6.5 0.0 copy-start
  6.5 0.0 all-gather.3.cloned.1.call-start
  6.5 0.7 all-gather.3.cloned.1.call-update
  7.3 0.0 all-gather.5.cloned.1.call-start
  7.3 0.9 subtract_bitcast_fusion
  8.2 78.9 %all-gather.3.cloned.1.call-done = bf16[65536,16]{0,1:T(8,128)(2,1)} async-done(((bf16[2048,16]{0,1:T(8,128)(2,1)}), bf16[65536,16]{0,1:T(8,128)(2,1)}) %all-gather.3.cloned.1.call-update) | async-done | bytes 2097168 | tf_op jit(solution)/shard_map/all_gather | solution.py:40
  87.1 3.1 %copy.26 = bf16[2,256,8,256]{3,2,0,1:T(8,128)(2,1)} copy(bf16[2,256,8,256]{3,2,1,0:T(8,128)(2,1)} %bitcast.49) | data formatting | bytes 4194304 | tf_op jit(solution)/shard_map/reshape | solution.py:41
  90.1 2.1 gather_fusion
  92.3 1.9 convolution_bitcast_fusion.2
  94.2 0.2 fusion.13
  94.4 0.6 copy.15
  95.0 0.0 all-gather.5.cloned.1.call-update
  95.1 68.9 %all-gather.5.cloned.1.call-done = bf16[65536,16]{0,1:T(8,128)(2,1)} async-done(((bf16[2048,16]{0,1:T(8,128)(2,1)}), bf16[65536,16]{0,1:T(8,128)(2,1)}) %all-gather.5.cloned.1.call-update) | async-done | bytes 2097168 | tf_op jit(solution)/shard_map/all_gather | solution.py:40
  164.0 3.1 %copy.25 = bf16[2,256,8,256]{3,2,0,1:T(8,128)(2,1)} copy(bf16[2,256,8,256]{3,2,1,0:T(8,128)(2,1)} %bitcast.50) | data formatting | bytes 4194304 | tf_op jit(solution)/shard_map/reshape | solution.py:41
  167.1 0.0 copy-start.1
  167.1 2.2 gather_fusion.1
  169.2 1.9 convolution_bitcast_fusion.1
  171.2 0.2 convolution_multiply_fusion
  171.4 0.0 copy-done.1
  171.4 0.1 broadcast_in_dim.2
  171.6 22.3 %all_to_all.10 = bf16[16,2048,16]{1,2,0:T(8,128)(2,1)S(1)} all-to-all(bf16[16,2048,16]{1,2,0:T(8,128)(2,1)S(1)} %broadcast_in_dim.2), channel_id=1, replica_groups=mesh['subj'=32,'var'=16] {'var'}, dimensions={0} | all-to-all | bytes 2097152 | tf_op jit(solution)/shard_map/all_to_all | solution.py:9
  193.8 0.0 copy-done
  193.8 1.9 convolution_bitcast_fusion
  195.7 2.3 copy.11
  198.0 54.9 %all_to_all.11 = f32[32,24,256]{2,1,0:T(8,128)} all-to-all(f32[32,24,256]{2,1,0:T(8,128)} %bitcast.48), channel_id=1, replica_groups=mesh['subj'=32,'var'=16] {'subj'}, dimensions={0} | all-to-all | bytes 1572864 | tf_op jit(solution)/shard_map/all_to_all | solution.py:31
  252.8 1.2 reduce_sum.9
  254.0 0.6 broadcast_multiply_fusion.1
  (4 shorter events, 0.1 us)
Async XLA Ops:
  6.5 187.3 %copy-start = (bf16[2048,768]{1,0:T(8,128)(2,1)S(1)}, bf16[2048,768]{1,0:T(8,128)(2,1)}, u32[]{:S(2)}) copy-start(bf16[2048,768]{1,0:T(8,128)(2,1)} %param.7) | copy-start | bytes 9437188
  6.5 80.5 %all-gather.3.cloned.1.call-start = ((), (), s32[]{:S(2)}) async-start(), calls=%async_computation.2 | async-start | bytes 2162688 | tf_op jit(solution)/shard_map/all_gather | solution.py:40
  7.3 156.7 %all-gather.5.cloned.1.call-start = ((), (), s32[]{:S(2)}) async-start(), calls=%async_computation.3 | async-start | bytes 2162688 | tf_op jit(solution)/shard_map/all_gather | solution.py:40
  167.1 4.3 %copy-start.1 = (bf16[2048,16]{0,1:T(8,128)(2,1)S(1)}, bf16[2048,16]{0,1:T(8,128)(2,1)}, u32[]{:S(2)}) copy-start(bf16[2048,16]{0,1:T(8,128)(2,1)} %param.4) | copy-start | bytes 196612
Sparse Core Ops, SparseCore 0:
  9.5 77.5 all-gather.2
  95.2 68.7 all-gather.4
where the time goes:
time: 262 us; the launch traced here: 261 us
  waiting for transfers between devices  149 us (57%)
  blocking collectives  77.1 us (29%)
  local copies, waits for them, and re-layouts  13.6 us (5%)
  between operations  13.5 us (5%)
  matrix products  6.06 us (2%)
  other arithmetic  2.72 us (1%)
    all_gather x2, waiting for transfers between devices, kinship_apply(): gathered = lax.all_gather(field, 'subj', axis=0, tiled=True)  148 us
    all_to_all x1, blocking collectives, sum_at_owner(): lax.all_to_all(blocks, axis, split_axis=0, concat_axis=0, tiled=True)  54.9 us
    all_to_all x1, blocking collectives, sent_to_all(): return lax.all_to_all(copies, axis, split_axis=0, concat_axis=0, tiled=True)  22.3 us
    reshape x2, local copies, waits for them, and re-layouts, kinship_apply(): slabs = gathered.reshape(-1, block, width)[kin_index[:, 1]]  6.13 us
  transfers between devices with their start and end apart: 2, of which 2 were waited for; matrix products, arithmetic and copies ran while one was open for 0% of the time, Pallas kernels for 0%

commit v1 on v0

v1 whole, which is shorter than its diff:
```python
import functools

import jax
import jax.numpy as jnp
from jax import lax
from jax.experimental import pallas as pl
from jax.experimental.pallas import tpu as pltpu
from jax.sharding import PartitionSpec as P

NEAR = 4
LANES = 128
VMEM = pl.BlockSpec(memory_space=pltpu.VMEM)
SMEM = pl.BlockSpec(memory_space=pltpu.SMEM)
PARAMS = pltpu.CompilerParams(vmem_limit_bytes=48 * 2**20)


def list_kernel(slots, here, index_ref, out_ref):
    me = lax.axis_index("subj")
    lane = lax.broadcasted_iota(jnp.int32, out_ref.shape[1:], 1)
    row = jnp.full(lane.shape, -1, jnp.int32)
    count = jnp.int32(0)
    for t in range(index_ref.shape[0]):
        col = index_ref[t, 1]
        remote = col // here != me
        row = jnp.where((lane == count) & remote, col, row)
        count = count + remote.astype(jnp.int32)
    for k in range(out_ref.shape[0]):
        out_ref[k] = row


def pack_kernel(slots, here, block, wanted_ref, near_ref, out_ref):
    group = lax.axis_index("subj") // NEAR
    for k in range(out_ref.shape[0]):
        for j in range(slots):
            col = wanted_ref[k, 0, j]

            @pl.when((col >= 0) & (col // (here * NEAR) == group))
            def _(k=k, j=j, col=col):
                inside = col - group * (here * NEAR)
                at = pl.multiple_of(inside % here * block, block)
                out_ref[k, j] = near_ref[inside // here, :, pl.ds(at, block)]


def apply_tiles(slots, here, block, index_ref, field_ref, far_ref, tiles_ref, sum_ref):
    me = lax.axis_index("subj")
    sum_ref[...] = jnp.zeros_like(sum_ref)
    count = jnp.int32(0)
    for t in range(tiles_ref.shape[0]):
        row = index_ref[t, 0] - me * here
        col = index_ref[t, 1]
        local = col // here == me
        at = pl.multiple_of(col % here * block, block)
        mine = field_ref[:, pl.ds(at, block)]
        other = far_ref[col // (here * NEAR), jnp.minimum(count, slots - 1)]
        count = count + jnp.where(local, 0, 1)
        slab = jnp.where(local, mine, other)
        prod = lax.dot_general(
            slab, tiles_ref[t], (((1,), (1,)), ((), ())), preferred_element_type=jnp.float32
        )
        to = pl.ds(pl.multiple_of(row * block, block), block)
        sum_ref[:, to] += prod


def first_kernel(slots, here, block, index_ref, field_ref, far_ref, tiles_ref, sum_ref, sent_ref):
    apply_tiles(slots, here, block, index_ref, field_ref, far_ref, tiles_ref, sum_ref)
    sent_ref[...] = sum_ref[...].astype(sent_ref.dtype)


def second_kernel(
    slots, here, block, index_ref, sent_ref, far_ref, tiles_ref, first_ref, traits_ref, out_ref, sum_ref
):
    apply_tiles(slots, here, block, index_ref, sent_ref, far_ref, tiles_ref, sum_ref)
    base = traits_ref[...].astype(jnp.float32)
    whitened = 0.6 * base + 0.5 * first_ref[...] + 0.3 * (2.0 * sum_ref[...] - base)
    whitened = whitened.astype(out_ref.dtype)
    for k in range(out_ref.shape[0]):
        out_ref[k] = whitened


def score_kernel(scale, wide_ref, dosages_ref, out_ref):
    cores, chips, rows, width = out_ref.shape
    step = 256
    for i in range(dosages_ref.shape[1] // step):
        part = jnp.dot(
            wide_ref[...], dosages_ref[:, i * step : (i + 1) * step], preferred_element_type=jnp.float32
        )
        part = part.T * scale
        for r in range(0, step, 8):
            at = i * step + r
            owner, inner = at // rows, at % rows
            out_ref[owner % cores, owner // cores, inner : inner + 8, :] = part[r : r + 8]


def add_kernel(mine_ref, other_ref, out_ref):
    out_ref[...] = mine_ref[...] + other_ref[...]


def sum_kernel(parts_ref, out_ref):
    total = parts_ref[0]
    for k in range(1, parts_ref.shape[0]):
        total = total + parts_ref[k]
    out_ref[...] = total


def call(kernel, out, specs, scratch=()):
    many = isinstance(out, list)
    return pl.pallas_call(
        kernel,
        out_shape=out,
        in_specs=specs,
        out_specs=[VMEM] * len(out) if many else VMEM,
        scratch_shapes=list(scratch),
        compiler_params=PARAMS,
    )


def on_device(traits, kin_tiles, kin_index, dosages):
    n = lax.axis_size("subj")
    m = lax.axis_size("var")
    rows_here, width = traits.shape
    tiles, block = kin_tiles.shape[:2]
    here = rows_here // block
    slots = tiles - here
    far = n // NEAR
    near_groups = [[k * NEAR + j for j in range(NEAR)] for k in range(far)]
    far_groups = [[k * NEAR + j for k in range(far)] for j in range(NEAR)]
    chip_groups = [list(range(c, n, 2)) for c in range(2)]
    f32, bf16 = jnp.float32, jnp.bfloat16
    sds = jax.ShapeDtypeStruct
    base = traits.T

    listed = call(
        functools.partial(list_kernel, slots, here), sds((far, 8, LANES), jnp.int32), [SMEM]
    )(kin_index)
    wanted = lax.all_to_all(listed, "subj", 0, 0, tiled=True, axis_index_groups=far_groups)
    wanted = wanted[:, :1, :8]

    def fetched(field):
        near = lax.all_gather(field, "subj", axis_index_groups=near_groups)
        packed = call(
            functools.partial(pack_kernel, slots, here, block),
            sds((far, slots, width, block), bf16),
            [SMEM, VMEM],
        )(wanted, near)
        return lax.all_to_all(packed, "subj", 0, 0, tiled=True, axis_index_groups=far_groups)

    first, sent = call(
        functools.partial(first_kernel, slots, here, block),
        [sds((width, rows_here), f32), sds((width, rows_here), bf16)],
        [SMEM, VMEM, VMEM, VMEM],
    )(kin_index, base, fetched(base), kin_tiles)
    copies = call(
        functools.partial(second_kernel, slots, here, block),
        sds((m, width, rows_here), bf16),
        [SMEM, VMEM, VMEM, VMEM, VMEM, VMEM],
        [pltpu.VMEM((width, rows_here), f32)],
    )(kin_index, sent, fetched(sent), kin_tiles, first, base)
    wide = lax.all_to_all(copies, "var", 0, 0, tiled=True).reshape(m * width, rows_here)

    scale = 1.0 / (127.5 * float(rows_here * n) ** 0.5)
    share = dosages.shape[1] // n
    parts = call(
        functools.partial(score_kernel, scale),
        sds((2, n // 2, share, m * width), f32),
        [VMEM, VMEM],
    )(wide, dosages)
    core = lax.axis_index("subj") % 2
    mine = lax.dynamic_index_in_dim(parts, core, 0, keepdims=False)
    other = lax.dynamic_index_in_dim(parts, 1 - core, 0, keepdims=False)
    other = lax.ppermute(other, "subj", [(s, s ^ 1) for s in range(n)])
    half = call(add_kernel, sds(mine.shape, f32), [VMEM, VMEM])(mine, other)
    arrived = lax.all_to_all(half, "subj", 0, 0, tiled=True, axis_index_groups=chip_groups)
    return call(sum_kernel, sds((share, m * width), f32), [VMEM])(arrived)


def solution(mesh):
    in_specs = (P("subj", "var"), P("subj", None, None), P("subj", None), P("subj", "var"))
    out_specs = P(("var", "subj"), None)
    return jax.shard_map(
        on_device, mesh=mesh, in_specs=in_specs, out_specs=out_specs, check_vma=False
    )
```

time: 262 us -> 154 us (0.59)
  the two profiles are of different devices: /device:TPU:1 before, /device:TPU:8 now
where the time goes in v1:
time: 154 us
  blocking collectives  90.3 us (59%)
  waiting for transfers between devices  25 us (16%)
  starting transfers between devices  24.4 us (16%)
  Pallas kernels  8.8 us (6%)
  local copies, waits for them, and re-layouts  5.01 us (3%)
    all_to_all x2, blocking collectives, fetched(): lax.all_to_all(packed, 'subj', 0, 0, tiled=True, axis_index_groups=far_gr...  51.1 us
    all_to_all x1, blocking collectives, on_device(): lax.all_to_all(half, 'subj', 0, 0, tiled=True, axis_index_groups=chip_gro...  27.1 us
    all_to_all x1, waiting for transfers between devices, on_device(): lax.all_to_all(copies, 'var', 0, 0, tiled=True)  16.6 us
    all_to_all x1, starting transfers between devices, on_device(): lax.all_to_all(listed, 'subj', 0, 0, tiled=True, axis_index_groups=far_gr...  15.1 us
    all_gather x2, blocking collectives, fetched(): near = lax.all_gather(field, 'subj', axis_index_groups=near_groups)  12 us
    all_to_all x1, starting transfers between devices, on_device(): lax.all_to_all(copies, 'var', 0, 0, tiled=True)  7.39 us
    all_to_all x1, waiting for transfers between devices, on_device(): lax.all_to_all(listed, 'subj', 0, 0, tiled=True, axis_index_groups=far_gr...  6.69 us
    unnamed x11, local copies, waits for them, and re-layouts  4.94 us
  transfers between devices with their start and end apart: 3, of which 3 were waited for; matrix products, arithmetic and copies ran while one was open for 0% of the time, Pallas kernels for 0%

profile of v1, /device:TPU:8, one launch (start us, length us, event | category | flops | bytes accessed | tf_op | source)
XLA Modules:
  0.0 153.6 jit_solution(8759943458943130008)
XLA Ops:
  0.0 0.0 copy-start.4
  0.0 0.8 copy.7.index_ref
  0.8 1.3 shard_map.46
  2.1 15.1 %all-to-all-start = ((s32[8,8,128]{2,1,0:T(8,128)}), s32[8,8,128]{2,1,0:T(8,128)S(1)}, u32[]{:S(2)}, u32[]{:S(2)}) async-start(s32[8,8,128]{2,1,0:T(8,128)} %shard_map.46), calls=%async_computation | async-start | bytes 65536 | tf_op jit(solution)/shard_map/all_to_all | solution.py:135
  17.2 6.2 %all-gather = bf16[64,2048]{1,0:T(8,128)(2,1)S(1)} all-gather(bf16[16,2048]{1,0:T(8,128)(2,1)} %bitcast.11), channel_id=2, replica_groups={{0,16,32,48},{64,80,96,112},{128,144,160,176},{192,208,224,240},{256,27..., dimensions={0}, use_global_device_ids=true | all-gather | bytes 327680 | tf_op jit(solution)/shard_map/all_gather | solution.py:139
  23.5 6.7 %all-to-all-done = s32[8,8,128]{2,1,0:T(8,128)S(1)} async-done(((s32[8,8,128]{2,1,0:T(8,128)}), s32[8,8,128]{2,1,0:T(8,128)S(1)}, u32[]{:S(2)}, u32[]{:S(2)}) %all-to-all-start) | async-done | bytes 32800 | tf_op jit(solution)/shard_map/all_to_all | solution.py:135
  30.2 1.1 shard_map.47
  31.3 26.7 %all_to_all.25.far_ref = bf16[8,4,16,256]{3,2,1,0:T(8,128)(2,1)S(1)} all-to-all(bf16[8,4,16,256]{3,2,1,0:T(8,128)(2,1)S(1)} %shard_map.47), channel_id=1, replica_groups={{0,64,128,192,256,320,384,448},{16,80,144,208,272,336,400,464},{32,96,1..., dimensions={0} | all-to-all | bytes 524288 | tf_op jit(solution)/shard_map/all_to_all | solution.py:145
  58.0 0.0 copy-start
  58.0 1.4 copy-done
  59.4 0.0 copy-start.3
  59.4 0.8 copy-done.3
  60.3 0.0 copy-start.1
  60.3 1.2 shard_map.48
  61.5 5.8 %all-gather.1 = bf16[64,2048]{1,0:T(8,128)(2,1)S(1)} all-gather(bf16[16,2048]{1,0:T(8,128)(2,1)S(1)} %get-tuple-element.7.sent_ref), channel_id=3, replica_groups={{0,16,32,48},{64,80,96,112},{128,144,160,176},{192,208,224,240},{256,27..., dimensions={0}, use_global_device_ids=true | all-gather | bytes 327680 | tf_op jit(solution)/shard_map/all_gather | solution.py:139
  67.3 1.1 shard_map.49
  68.4 24.4 %all_to_all.26.far_ref = bf16[8,4,16,256]{3,2,1,0:T(8,128)(2,1)S(1)} all-to-all(bf16[8,4,16,256]{3,2,1,0:T(8,128)(2,1)S(1)} %shard_map.49), channel_id=1, replica_groups={{0,64,128,192,256,320,384,448},{16,80,144,208,272,336,400,464},{32,96,1..., dimensions={0} | all-to-all | bytes 524288 | tf_op jit(solution)/shard_map/all_to_all | solution.py:145
  92.8 0.0 copy-done.4
  92.8 0.0 copy-done.1
  92.8 2.3 %shard_map.50 = bf16[16,16,2048]{2,1,0:T(8,128)(2,1)} custom-call(s32[12,2]{1,0:T(8,128)S(1)} %copy.7.index_ref, bf16[16,2048]{1,0:T(8,128)(2,1)S(1)} %get-tuple-element.7.sent_ref, bf16[8,4,16,256]{3,2,1,0:T(8,128)(2,1)S(1)} %all_to_all.26.far_ref, bf16[12,256,256]{2,1,0:T(8,128)(2,1)S(1)} %copy-done.1, f32[16,2048]{1,0:T(8,128)S(1)} %get-tuple-element.8.first_ref, ...), custom_call_target="tpu_custom_call" | custom-call | tf_op jit(solution)/shard_map/pallas_call | solution.py:152
  95.0 7.4 %all-to-all-start.3 = ((bf16[16,16,2048]{2,1,0:T(8,128)(2,1)}), bf16[16,16,2048]{2,1,0:T(8,128)(2,1)S(1)}, u32[]{:S(2)}, u32[]{:S(2)}) async-start(bf16[16,16,2048]{2,1,0:T(8,128)(2,1)} %shard_map.50), calls=%async_computation.3 | async-start | bytes 2097152 | tf_op jit(solution)/shard_map/all_to_all | solution.py:158
  102.4 16.6 %all-to-all-done.3 = bf16[16,16,2048]{2,1,0:T(8,128)(2,1)S(1)} async-done(((bf16[16,16,2048]{2,1,0:T(8,128)(2,1)}), bf16[16,16,2048]{2,1,0:T(8,128)(2,1)S(1)}, u32[]{:S(2)}, u32[]{:S(2)}) %all-to-all-start.3) | async-done | bytes 1048608 | tf_op jit(solution)/shard_map/all_to_all | solution.py:158
  119.1 0.0 copy-start.2
  119.1 1.9 %copy-done.2 = bf16[2048,768]{1,0:T(8,128)(2,1)S(1)} copy-done((bf16[2048,768]{1,0:T(8,128)(2,1)S(1)}, bf16[2048,768]{1,0:T(8,128)(2,1)}, u32[]{:S(2)}) %copy-start.2) | copy-done | bytes 3145752
  121.0 1.1 shard_map.51
  122.1 0.1 dynamic-slice_bitcast_fusion
  122.2 1.9 %collective-permute-start = (f32[16,24,256]{2,1,0:T(8,128)S(1)}, f32[16,24,256]{2,1,0:T(8,128)S(1)}, u32[]{:S(2)}, u32[]{:S(2)}) collective-permute-start(f32[16,24,256]{2,1,0:T(8,128)S(1)} %get-tuple-element.9), channel_id=1, source_target_pairs={{0,16},{16,0},{32,48},{48,32},{64,80},{80,64},{96,112},{112,96},{1... | collective-permute-start | bytes 1179656 | tf_op jit(solution)/shard_map/ppermute | solution.py:170
  124.1 1.7 %collective-permute-done.other_ref = f32[16,24,256]{2,1,0:T(8,128)S(1)} collective-permute-done((f32[16,24,256]{2,1,0:T(8,128)S(1)}, f32[16,24,256]{2,1,0:T(8,128)S(1)}, u32[]{:S(2)}, u32[]{:S(2)}) %collective-permute-start) | collective-permute-done | bytes 393248 | tf_op jit(solution)/shard_map/ppermute | solution.py:170
  125.8 27.1 %all_to_all.27.parts_ref = f32[16,24,256]{2,1,0:T(8,128)S(1)} all-to-all(f32[16,24,256]{2,1,0:T(8,128)S(1)} %shard_map.52), channel_id=1, replica_groups={{0,32,64,96,128,160,192,224,256,288,320,352,384,416,448,480},{16,48,80,..., dimensions={0} | all-to-all | bytes 786432 | tf_op jit(solution)/shard_map/all_to_all | solution.py:172
  152.9 0.6 shard_map.53
  (2 shorter events, 0.0 us)
Async XLA Ops:
  0.0 92.8 %copy-start.4 = (bf16[2048,16]{0,1:T(8,128)(2,1)S(1)}, bf16[2048,16]{0,1:T(8,128)(2,1)}, u32[]{:S(2)}) copy-start(bf16[2048,16]{0,1:T(8,128)(2,1)} %param.4) | copy-start | bytes 196612
  2.1 28.0 %all-to-all-start = ((s32[8,8,128]{2,1,0:T(8,128)}), s32[8,8,128]{2,1,0:T(8,128)S(1)}, u32[]{:S(2)}, u32[]{:S(2)}) async-start(s32[8,8,128]{2,1,0:T(8,128)} %shard_map.46), calls=%async_computation | async-start | bytes 65536 | tf_op jit(solution)/shard_map/all_to_all | solution.py:135
  58.0 1.4 copy-start
  59.4 0.8 copy-start.3
  60.3 32.5 %copy-start.1 = (bf16[12,256,256]{2,1,0:T(8,128)(2,1)S(1)}, bf16[12,256,256]{2,1,0:T(8,128)(2,1)}, u32[]{:S(2)}) copy-start(bf16[12,256,256]{2,1,0:T(8,128)(2,1)} %tiles_ref.3) | copy-start | bytes 4718596
  95.0 24.0 %all-to-all-start.3 = ((bf16[16,16,2048]{2,1,0:T(8,128)(2,1)}), bf16[16,16,2048]{2,1,0:T(8,128)(2,1)S(1)}, u32[]{:S(2)}, u32[]{:S(2)}) async-start(bf16[16,16,2048]{2,1,0:T(8,128)(2,1)} %shard_map.50), calls=%async_computation.3 | async-start | bytes 2097152 | tf_op jit(solution)/shard_map/all_to_all | solution.py:158
  119.1 1.9 %copy-start.2 = (bf16[2048,768]{1,0:T(8,128)(2,1)S(1)}, bf16[2048,768]{1,0:T(8,128)(2,1)}, u32[]{:S(2)}) copy-start(bf16[2048,768]{1,0:T(8,128)(2,1)} %dosages_ref.1) | copy-start | bytes 9437188
  122.2 3.6 %collective-permute-start = (f32[16,24,256]{2,1,0:T(8,128)S(1)}, f32[16,24,256]{2,1,0:T(8,128)S(1)}, u32[]{:S(2)}, u32[]{:S(2)}) collective-permute-start(f32[16,24,256]{2,1,0:T(8,128)S(1)} %get-tuple-element.9), channel_id=1, source_target_pairs={{0,16},{16,0},{32,48},{48,32},{64,80},{80,64},{96,112},{112,96},{1... | collective-permute-start | bytes 1179656 | tf_op jit(solution)/shard_map/ppermute | solution.py:170

commit v2 on v1

v2 whole, which is shorter than its diff:
```python
import functools

import jax
import jax.numpy as jnp
from jax import lax
from jax.experimental import pallas as pl
from jax.experimental.pallas import tpu as pltpu
from jax.sharding import PartitionSpec as P

NEAR = 4
LANES = 128
NONE = 256
VMEM = pl.BlockSpec(memory_space=pltpu.VMEM)
ANY = pl.BlockSpec(memory_space=pl.ANY)
SMEM = pl.BlockSpec(memory_space=pltpu.SMEM)
PARAMS = pltpu.CompilerParams(vmem_limit_bytes=48 * 2**20)


def send_kernel(here, index_ref, field_ref, out_ref):
    me = lax.axis_index("subj")
    rows_here = field_ref.shape[1]
    shape = (field_ref.shape[0], out_ref.shape[2] - rows_here)
    lane = lax.broadcasted_iota(jnp.int32, shape, 1)
    listed = jnp.full(shape, NONE, jnp.int32)
    count = jnp.int32(0)
    for t in range(index_ref.shape[1]):
        col = index_ref[1, t]
        remote = jnp.where(col // here != me, 1, 0)
        listed = jnp.where(lane == jnp.where(remote == 1, count, -1), col, listed)
        count = count + remote
    listed = listed.astype(jnp.float32).astype(out_ref.dtype)
    for k in range(out_ref.shape[0]):
        out_ref[k, :, :rows_here] = field_ref[...]
        out_ref[k, :, rows_here:] = listed


def pack_near_kernel(slots, here, block, index_ref, far_ref, out_ref):
    me = lax.axis_index("subj")
    group, inner = me // NEAR, me % NEAR
    for p in range(NEAR):
        count = jnp.int32(0)
        for t in range(index_ref.shape[2]):
            col = index_ref[p, 1, t]
            owner = col // here
            remote = owner != group * NEAR + p

            @pl.when(remote & (owner % NEAR == inner))
            def _(p=p, col=col, owner=owner, count=count):
                at = pl.multiple_of(col % here * block, block)
                out_ref[p, jnp.minimum(count, slots - 1)] = far_ref[owner // NEAR, :, pl.ds(at, block)]

            count = count + jnp.where(remote, 1, 0)


def pack_far_kernel(slots, here, block, wanted_ref, near_ref, out_ref):
    group = lax.axis_index("subj") // NEAR
    for k in range(out_ref.shape[0]):
        for j in range(slots):
            col = wanted_ref[k, j]

            @pl.when((col < NONE) & (col // (here * NEAR) == group))
            def _(k=k, j=j, col=col):
                inside = col - group * (here * NEAR)
                at = pl.multiple_of(inside % here * block, block)
                out_ref[k, j] = near_ref[inside // here, :, pl.ds(at, block)]


def apply_tiles(slots, here, block, source, index_ref, field_ref, other_ref, tile, sum_ref):
    me = lax.axis_index("subj")
    inner = me % NEAR
    sum_ref[...] = jnp.zeros_like(sum_ref)
    count = jnp.int32(0)
    for t in range(index_ref.shape[2]):
        row = index_ref[inner, 0, t] - me * here
        col = index_ref[inner, 1, t]
        local = col // here == me
        at = pl.multiple_of(col % here * block, block)
        mine = field_ref[:, pl.ds(at, block)]
        other = other_ref[source(col), jnp.minimum(count, slots - 1)]
        count = count + jnp.where(local, 0, 1)
        slab = jnp.where(local, mine, other)
        prod = lax.dot_general(
            slab, tile(t), (((1,), (1,)), ((), ())), preferred_element_type=jnp.float32
        )
        to = pl.ds(pl.multiple_of(row * block, block), block)
        sum_ref[:, to] += prod


def first_kernel(
    slots, here, block, index_ref, far_ref, other_ref, tiles_ref, sum_ref, sent_ref, held, sems
):
    copies = [
        pltpu.make_async_copy(tiles_ref.at[t], held.at[t], sems.at[t]) for t in range(held.shape[0])
    ]
    for copy in copies:
        copy.start()

    def tile(t):
        copies[t].wait()
        return held[t]

    def source(col):
        return col // here % NEAR

    own = far_ref.at[lax.axis_index("subj") // NEAR]
    apply_tiles(slots, here, block, source, index_ref, own, other_ref, tile, sum_ref)
    sent_ref[...] = sum_ref[...].astype(sent_ref.dtype)


def second_kernel(
    slots, here, block, index_ref, sent_ref, other_ref, tiles_ref, first_ref, far_ref, out_ref, sum_ref
):
    def source(col):
        return col // (here * NEAR)

    def tile(t):
        return tiles_ref[t]

    apply_tiles(slots, here, block, source, index_ref, sent_ref, other_ref, tile, sum_ref)
    rows_here = sum_ref.shape[1]
    base = far_ref[lax.axis_index("subj") // NEAR, :, :rows_here].astype(jnp.float32)
    whitened = 0.6 * base + 0.5 * first_ref[...] + 0.3 * (2.0 * sum_ref[...] - base)
    whitened = whitened.astype(out_ref.dtype)
    for k in range(out_ref.shape[0]):
        out_ref[k] = whitened


def score_kernel(scale, wide_ref, dosages_ref, out_ref, held, sems):
    core = lax.axis_index("subj") % 2
    rows = out_ref.shape[2]
    steps, _, step = held.shape
    copies = [
        pltpu.make_async_copy(
            dosages_ref.at[:, i * step : (i + 1) * step], held.at[i], sems.at[i]
        )
        for i in range(steps)
    ]
    for copy in copies:
        copy.start()
    for i in range(steps):
        copies[i].wait()
        part = jnp.dot(wide_ref[...], held[i], preferred_element_type=jnp.float32)
        part = part.T * scale
        for r in range(0, step, 8):
            owner, inner = divmod(i * step + r, rows)
            out_ref[core if owner % 2 == 0 else 1 - core, owner // 2, inner : inner + 8, :] = part[r : r + 8]


def add_kernel(mine_ref, other_ref, out_ref):
    out_ref[...] = mine_ref[...] + other_ref[...]


def sum_kernel(parts_ref, out_ref):
    total = parts_ref[0]
    for k in range(1, parts_ref.shape[0]):
        total = total + parts_ref[k]
    out_ref[...] = total


def call(kernel, out, specs, scratch=()):
    many = isinstance(out, list)
    return pl.pallas_call(
        kernel,
        out_shape=out,
        in_specs=specs,
        out_specs=[VMEM] * len(out) if many else VMEM,
        scratch_shapes=list(scratch),
        compiler_params=PARAMS,
    )


def on_device(traits, kin_tiles, kin_index, dosages):
    n = lax.axis_size("subj")
    m = lax.axis_size("var")
    rows_here, width = traits.shape
    tiles, block = kin_tiles.shape[:2]
    here = rows_here // block
    slots = tiles - here
    far = n // NEAR
    near_groups = [[k * NEAR + j for j in range(NEAR)] for k in range(far)]
    far_groups = [[k * NEAR + j for k in range(far)] for j in range(NEAR)]
    chip_groups = [list(range(c, n, 2)) for c in range(2)]
    f32, bf16 = jnp.float32, jnp.bfloat16
    sds = jax.ShapeDtypeStruct
    base = traits.T
    index = kin_index.T

    out = call(
        functools.partial(send_kernel, here), sds((far, width, rows_here + LANES), bf16), [SMEM, VMEM]
    )(index, base)
    dense = lax.all_to_all(out, "subj", 0, 0, tiled=True, axis_index_groups=far_groups)
    near_index = lax.all_gather(index, "subj", axis_index_groups=near_groups)
    wanted = dense[:, 0, rows_here : rows_here + slots].astype(jnp.int32)
    packed = call(
        functools.partial(pack_near_kernel, slots, here, block),
        sds((NEAR, slots, width, block), bf16),
        [SMEM, VMEM],
    )(near_index, dense)
    arrived = lax.all_to_all(packed, "subj", 0, 0, tiled=True, axis_index_groups=near_groups)
    first, sent = call(
        functools.partial(first_kernel, slots, here, block),
        [sds((width, rows_here), f32), sds((width, rows_here), bf16)],
        [SMEM, VMEM, VMEM, ANY],
        [pltpu.VMEM(kin_tiles.shape, bf16), pltpu.SemaphoreType.DMA((tiles,))],
    )(near_index, dense, arrived, kin_tiles)

    near = lax.all_gather(sent, "subj", axis_index_groups=near_groups)
    packed = call(
        functools.partial(pack_far_kernel, slots, here, block),
        sds((far, slots, width, block), bf16),
        [SMEM, VMEM],
    )(wanted, near)
    arrived = lax.all_to_all(packed, "subj", 0, 0, tiled=True, axis_index_groups=far_groups)
    copies = call(
        functools.partial(second_kernel, slots, here, block),
        sds((m, width, rows_here), bf16),
        [SMEM, VMEM, VMEM, VMEM, VMEM, VMEM],
        [pltpu.VMEM((width, rows_here), f32)],
    )(near_index, sent, arrived, kin_tiles, first, dense)
    wide = lax.all_to_all(copies, "var", 0, 0, tiled=True).reshape(m * width, rows_here)

    scale = 1.0 / (127.5 * float(rows_here * n) ** 0.5)
    share = dosages.shape[1] // n
    step = 256
    parts = call(
        functools.partial(score_kernel, scale),
        sds((2, n // 2, share, m * width), f32),
        [VMEM, ANY],
        [
            pltpu.VMEM((dosages.shape[1] // step, rows_here, step), bf16),
            pltpu.SemaphoreType.DMA((dosages.shape[1] // step,)),
        ],
    )(wide, dosages)
    mine = parts[0]
    other = lax.ppermute(parts[1], "subj", [(s, s ^ 1) for s in range(n)])
    half = call(add_kernel, sds(mine.shape, f32), [VMEM, VMEM])(mine, other)
    arrived = lax.all_to_all(half, "subj", 0, 0, tiled=True, axis_index_groups=chip_groups)
    return call(sum_kernel, sds((share, m * width), f32), [VMEM])(arrived)


def solution(mesh):
    in_specs = (P("subj", "var"), P("subj", None, None), P("subj", None), P("subj", "var"))
    out_specs = P(("var", "subj"), None)
    return jax.shard_map(
        on_device, mesh=mesh, in_specs=in_specs, out_specs=out_specs, check_vma=False
    )
```

time: 154 us -> 157 us (1.019)
  blocking collectives: 90.3 us -> 99.1 us
  Pallas kernels: 8.8 us -> 13.9 us
  starting transfers between devices: 24.4 us -> 20.3 us
  local copies, waits for them, and re-layouts: 5.01 us -> 1.7 us
  waiting for transfers between devices: 25 us -> 21.9 us
    all_gather x2, blocking collectives: 12 us -> 24.6 us  [the longest x1 18.9 us: on_device(): near_index = lax.all_gather(index, 'subj', axis_index_groups=near_groups)]
    all_to_all x2, starting transfers between devices: 22.5 us -> 18.4 us  [the longest x1 15.1 us: on_device(): lax.all_to_all(out, 'subj', 0, 0, tiled=True, axis_index_groups=far_groups)]
    pallas_call x1, Pallas kernels: 1.2 us -> 5 us  [on_device(): call(functools.partial(first_kernel, slots, here, block), [sds((width, ro...]
    all_to_all x2, blocking collectives: 51.1 us -> 47.4 us  [the longest x1 24.3 us: on_device(): lax.all_to_all(packed, 'subj', 0, 0, tiled=True, axis_index_groups=far_gr...]
    unnamed x11 -> x8, local copies, waits for them, and re-layouts: 4.94 us -> 1.65 us
    all_to_all x2, waiting for transfers between devices: 23.3 us -> 20.2 us  [the longest x1 15.7 us: on_device(): lax.all_to_all(out, 'subj', 0, 0, tiled=True, axis_index_groups=far_groups)]
where the time goes in v2:
time: 157 us
  blocking collectives  99.1 us (63%)
  waiting for transfers between devices  21.9 us (14%)
  starting transfers between devices  20.3 us (13%)
  Pallas kernels  13.9 us (9%)
  local copies, waits for them, and re-layouts  1.7 us (1%)
    all_to_all x1, blocking collectives, on_device(): lax.all_to_all(half, 'subj', 0, 0, tiled=True, axis_index_groups=chip_gro...  27 us
    all_to_all x1, blocking collectives, on_device(): lax.all_to_all(packed, 'subj', 0, 0, tiled=True, axis_index_groups=far_gr...  24.3 us
    all_to_all x1, blocking collectives, on_device(): lax.all_to_all(copies, 'var', 0, 0, tiled=True)  23.2 us
    all_gather x1, blocking collectives, on_device(): near_index = lax.all_gather(index, 'subj', axis_index_groups=near_groups)  18.9 us
    all_to_all x1, waiting for transfers between devices, on_device(): lax.all_to_all(out, 'subj', 0, 0, tiled=True, axis_index_groups=far_groups)  15.7 us
    all_to_all x1, starting transfers between devices, on_device(): lax.all_to_all(out, 'subj', 0, 0, tiled=True, axis_index_groups=far_groups)  15.1 us
    all_gather x1, blocking collectives, on_device(): near = lax.all_gather(sent, 'subj', axis_index_groups=near_groups)  5.79 us
    pallas_call x1, Pallas kernels, on_device(): call(functools.partial(first_kernel, slots, here, block), [sds((width, ro...  5 us
  transfers between devices with their start and end apart: 3, of which 3 were waited for; matrix products, arithmetic and copies ran while one was open for 0% of the time, Pallas kernels for 0%

profile of v2, /device:TPU:8, one launch (start us, length us, event | category | flops | bytes accessed | tf_op | source)
XLA Modules:
  0.0 157.1 jit_solution(16014174213062167358)
XLA Ops:
  0.0 0.0 copy-start
  0.0 0.0 copy-start.2
  0.0 1.0 copy-done.2
  1.0 0.0 copy-start.3
  1.0 0.7 copy-done.3
  1.6 1.4 shard_map.46
  3.1 15.1 %all-to-all-start = ((bf16[8,16,2176]{2,1,0:T(8,128)(2,1)}), bf16[8,16,2176]{2,1,0:T(8,128)(2,1)S(1)}, u32[]{:S(2)}, u32[]{:S(2)}) async-start(bf16[8,16,2176]{2,1,0:T(8,128)(2,1)} %shard_map.46), calls=%async_computation | async-start | bytes 1114112 | tf_op jit(solution)/shard_map/all_to_all | solution.py:191
  18.2 18.9 %all-gather.2.index_ref = s32[4,2,12]{2,1,0:T(2,128)S(1)} all-gather(s32[1,2,12]{2,1,0:T(2,128)} %bitcast.15), channel_id=2, replica_groups={{0,16,32,48},{64,80,96,112},{128,144,160,176},{192,208,224,240},{256,27..., dimensions={0}, use_global_device_ids=true | all-gather | bytes 480 | tf_op jit(solution)/shard_map/all_gather | solution.py:192
  37.0 15.7 %all-to-all-done.far_ref = bf16[8,16,2176]{2,1,0:T(8,128)(2,1)S(1)} async-done(((bf16[8,16,2176]{2,1,0:T(8,128)(2,1)}), bf16[8,16,2176]{2,1,0:T(8,128)(2,1)S(1)}, u32[]{:S(2)}, u32[]{:S(2)}) %all-to-all-start) | async-done | bytes 557088 | tf_op jit(solution)/shard_map/all_to_all | solution.py:191
  52.7 2.2 %shard_map.47 = bf16[4,4,16,256]{3,2,1,0:T(8,128)(2,1)} custom-call(s32[4,2,12]{2,1,0:T(2,128)S(1)} %all-gather.2.index_ref, bf16[8,16,2176]{2,1,0:T(8,128)(2,1)S(1)} %all-to-all-done.far_ref), custom_call_target="tpu_custom_call" | custom-call | tf_op jit(solution)/shard_map/pallas_call | solution.py:194
  54.9 3.3 %all-to-all-start.1 = ((bf16[4,4,16,256]{3,2,1,0:T(8,128)(2,1)}), bf16[4,4,16,256]{3,2,1,0:T(8,128)(2,1)S(1)}, u32[]{:S(2)}, u32[]{:S(2)}) async-start(bf16[4,4,16,256]{3,2,1,0:T(8,128)(2,1)} %shard_map.47), calls=%async_computation.1 | async-start | bytes 262144 | tf_op jit(solution)/shard_map/all_to_all | solution.py:199
  58.2 4.6 %all-to-all-done.1.other_ref = bf16[4,4,16,256]{3,2,1,0:T(8,128)(2,1)S(1)} async-done(((bf16[4,4,16,256]{3,2,1,0:T(8,128)(2,1)}), bf16[4,4,16,256]{3,2,1,0:T(8,128)(2,1)S(1)}, u32[]{:S(2)}, u32[]{:S(2)}) %all-to-all-start.1) | async-done | bytes 131104 | tf_op jit(solution)/shard_map/all_to_all | solution.py:199
  62.8 0.0 copy-done
  62.8 5.0 %shard_map.48 = (f32[16,2048]{1,0:T(8,128)S(1)}, bf16[16,2048]{1,0:T(8,128)(2,1)S(1)}) custom-call(s32[4,2,12]{2,1,0:T(2,128)S(1)} %all-gather.2.index_ref, bf16[8,16,2176]{2,1,0:T(8,128)(2,1)S(1)} %all-to-all-done.far_ref, bf16[4,4,16,256]{3,2,1,0:T(8,128)(2,1)S(1)} %all-to-all-done.1.other_ref, bf16[12,256,256]{2,1,0:T(8,128)(2,1)S(1)} %copy-done), custom_call_target="tpu_custom_call" | custom-call | tf_op jit(solution)/shard_map/pallas_call | solution.py:200
  67.8 5.8 %all-gather.1 = bf16[64,2048]{1,0:T(8,128)(2,1)S(1)} all-gather(bf16[16,2048]{1,0:T(8,128)(2,1)S(1)} %get-tuple-element.7.sent_ref), channel_id=3, replica_groups={{0,16,32,48},{64,80,96,112},{128,144,160,176},{192,208,224,240},{256,27..., dimensions={0}, use_global_device_ids=true | all-gather | bytes 327680 | tf_op jit(solution)/shard_map/all_gather | solution.py:207
  73.6 1.1 shard_map.49
  74.7 0.0 copy-start.1
  74.7 24.3 %all_to_all.25.other_ref = bf16[8,4,16,256]{3,2,1,0:T(8,128)(2,1)S(1)} all-to-all(bf16[8,4,16,256]{3,2,1,0:T(8,128)(2,1)S(1)} %shard_map.49), channel_id=1, replica_groups={{0,64,128,192,256,320,384,448},{16,80,144,208,272,336,400,464},{32,96,1..., dimensions={0} | all-to-all | bytes 524288 | tf_op jit(solution)/shard_map/all_to_all | solution.py:213
  99.0 1.2 shard_map.50
  100.2 23.2 %all_to_all.26 = bf16[16,16,2048]{2,1,0:T(8,128)(2,1)S(1)} all-to-all(bf16[16,16,2048]{2,1,0:T(8,128)(2,1)S(1)} %shard_map.50), channel_id=1, replica_groups=mesh['subj'=32,'var'=16] {'var'}, dimensions={0} | all-to-all | bytes 2097152 | tf_op jit(solution)/shard_map/all_to_all | solution.py:220
  123.4 0.0 copy-done.1
  123.4 2.3 %shard_map.51 = f32[2,16,24,256]{3,2,1,0:T(8,128)S(1)} custom-call(bf16[256,2048]{1,0:T(8,128)(2,1)S(1)} %bitcast.11, bf16[2048,768]{1,0:T(8,128)(2,1)S(1)} %copy-done.1), custom_call_target="tpu_custom_call" | custom-call | tf_op jit(solution)/shard_map/pallas_call | solution.py:225
  125.6 0.1 slice_bitcast_fusion
  125.7 1.9 %collective-permute-start = (f32[16,24,256]{2,1,0:T(8,128)S(1)}, f32[16,24,256]{2,1,0:T(8,128)S(1)}, u32[]{:S(2)}, u32[]{:S(2)}) collective-permute-start(f32[16,24,256]{2,1,0:T(8,128)S(1)} %get-tuple-element.9), channel_id=1, source_target_pairs={{0,16},{16,0},{32,48},{48,32},{64,80},{80,64},{96,112},{112,96},{1... | collective-permute-start | bytes 1179656 | tf_op jit(solution)/shard_map/ppermute | solution.py:235
  127.6 1.7 %collective-permute-done.other_ref = f32[16,24,256]{2,1,0:T(8,128)S(1)} collective-permute-done((f32[16,24,256]{2,1,0:T(8,128)S(1)}, f32[16,24,256]{2,1,0:T(8,128)S(1)}, u32[]{:S(2)}, u32[]{:S(2)}) %collective-permute-start) | collective-permute-done | bytes 393248 | tf_op jit(solution)/shard_map/ppermute | solution.py:235
  129.4 27.0 %all_to_all.27.parts_ref = f32[16,24,256]{2,1,0:T(8,128)S(1)} all-to-all(f32[16,24,256]{2,1,0:T(8,128)S(1)} %shard_map.52), channel_id=1, replica_groups={{0,32,64,96,128,160,192,224,256,288,320,352,384,416,448,480},{16,48,80,..., dimensions={0} | all-to-all | bytes 786432 | tf_op jit(solution)/shard_map/all_to_all | solution.py:237
  156.4 0.6 shard_map.53
  (2 shorter events, 0.0 us)
Async XLA Ops:
  0.0 62.8 %copy-start = (bf16[12,256,256]{2,1,0:T(8,128)(2,1)S(1)}, bf16[12,256,256]{2,1,0:T(8,128)(2,1)}, u32[]{:S(2)}) copy-start(bf16[12,256,256]{2,1,0:T(8,128)(2,1)} %tiles_ref.3) | copy-start | bytes 4718596
  0.0 1.0 copy-start.2
  1.0 0.7 copy-start.3
  3.1 49.6 %all-to-all-start = ((bf16[8,16,2176]{2,1,0:T(8,128)(2,1)}), bf16[8,16,2176]{2,1,0:T(8,128)(2,1)S(1)}, u32[]{:S(2)}, u32[]{:S(2)}) async-start(bf16[8,16,2176]{2,1,0:T(8,128)(2,1)} %shard_map.46), calls=%async_computation | async-start | bytes 1114112 | tf_op jit(solution)/shard_map/all_to_all | solution.py:191
  54.9 7.9 %all-to-all-start.1 = ((bf16[4,4,16,256]{3,2,1,0:T(8,128)(2,1)}), bf16[4,4,16,256]{3,2,1,0:T(8,128)(2,1)S(1)}, u32[]{:S(2)}, u32[]{:S(2)}) async-start(bf16[4,4,16,256]{3,2,1,0:T(8,128)(2,1)} %shard_map.47), calls=%async_computation.1 | async-start | bytes 262144 | tf_op jit(solution)/shard_map/all_to_all | solution.py:199
  74.7 48.7 %copy-start.1 = (bf16[2048,768]{1,0:T(8,128)(2,1)S(1)}, bf16[2048,768]{1,0:T(8,128)(2,1)}, u32[]{:S(2)}) copy-start(bf16[2048,768]{1,0:T(8,128)(2,1)} %dosages_ref.1) | copy-start | bytes 9437188
  125.7 3.6 %collective-permute-start = (f32[16,24,256]{2,1,0:T(8,128)S(1)}, f32[16,24,256]{2,1,0:T(8,128)S(1)}, u32[]{:S(2)}, u32[]{:S(2)}) collective-permute-start(f32[16,24,256]{2,1,0:T(8,128)S(1)} %get-tuple-element.9), channel_id=1, source_target_pairs={{0,16},{16,0},{32,48},{48,32},{64,80},{80,64},{96,112},{112,96},{1... | collective-permute-start | bytes 1179656 | tf_op jit(solution)/shard_map/ppermute | solution.py:235

commit v3 on v1

v3 whole, which is shorter than its diff:
```python
import functools

import jax
import jax.numpy as jnp
from jax import lax
from jax.experimental import pallas as pl
from jax.experimental.pallas import tpu as pltpu
from jax.sharding import PartitionSpec as P

NEAR_TRAITS, NEAR_FIRST = 8, 4
LANES = 128
NONE = -1
VMEM = pl.BlockSpec(memory_space=pltpu.VMEM)
SMEM = pl.BlockSpec(memory_space=pltpu.SMEM)
PARAMS = pltpu.CompilerParams(vmem_limit_bytes=48 * 2**20)


def list_kernel(here, index_ref, out_ref):
    me = lax.axis_index("subj")
    shape = out_ref.shape[1:]
    lane = lax.broadcasted_iota(jnp.int32, shape, 1)
    line = lax.broadcasted_iota(jnp.int32, shape, 0)
    listed = jnp.full(shape, NONE, jnp.int32)
    count = jnp.int32(0)
    for t in range(index_ref.shape[1]):
        row, col = index_ref[0, t], index_ref[1, t]
        remote = jnp.where(col // here != me, 1, 0)
        listed = jnp.where((line == 0) & (lane == jnp.where(remote == 1, count, -1)), col, listed)
        listed = jnp.where((line == 1) & (lane == t), row, listed)
        listed = jnp.where((line == 2) & (lane == t), col, listed)
        count = count + remote
    for k in range(out_ref.shape[0]):
        out_ref[k] = listed


def pack_kernel(group, here, block, lists_ref, near_ref, out_ref):
    me = lax.axis_index("subj")
    near = near_ref.shape[0]
    for k in range(out_ref.shape[0]):
        partner = (k * near + me % near) // group
        for j in range(out_ref.shape[1]):
            col = lists_ref[partner, 0, j]

            @pl.when((col >= 0) & (col // (here * near) == me // near))
            def _(k=k, j=j, col=col):
                inside = col - me // near * (here * near)
                at = pl.multiple_of(inside % here * block, block)
                out_ref[k, j] = near_ref[inside // here, :, pl.ds(at, block)]


def apply_tiles(group, here, block, lists_ref, field_ref, other_ref, tiles_ref, sum_ref):
    me = lax.axis_index("subj")
    sources, slots = other_ref.shape[:2]
    held = lax.axis_size("subj") // sources * here
    sum_ref[...] = jnp.zeros_like(sum_ref)
    count = jnp.int32(0)
    for t in range(tiles_ref.shape[0]):
        row = lists_ref[me // group, 1, t] - me * here
        col = lists_ref[me // group, 2, t]
        local = col // here == me
        at = pl.multiple_of(col % here * block, block)
        mine = field_ref[:, pl.ds(at, block)]
        other = other_ref[col // held, jnp.minimum(count, slots - 1)]
        count = count + jnp.where(local, 0, 1)
        slab = jnp.where(local, mine, other)
        prod = lax.dot_general(
            slab, tiles_ref[t], (((1,), (1,)), ((), ())), preferred_element_type=jnp.float32
        )
        to = pl.ds(pl.multiple_of(row * block, block), block)
        sum_ref[:, to] += prod


def first_kernel(
    group, here, block, lists_ref, near_ref, other_ref, tiles_ref, sum_ref, sent_ref
):
    own = near_ref.at[lax.axis_index("subj") % near_ref.shape[0]]
    apply_tiles(group, here, block, lists_ref, own, other_ref, tiles_ref, sum_ref)
    sent_ref[...] = sum_ref[...].astype(sent_ref.dtype)


def second_kernel(
    group, here, block, lists_ref, sent_ref, other_ref, tiles_ref, first_ref, near_ref, out_ref, sum_ref
):
    apply_tiles(group, here, block, lists_ref, sent_ref, other_ref, tiles_ref, sum_ref)
    base = near_ref[lax.axis_index("subj") % near_ref.shape[0]].astype(jnp.float32)
    whitened = 0.6 * base + 0.5 * first_ref[...] + 0.3 * (2.0 * sum_ref[...] - base)
    whitened = whitened.astype(out_ref.dtype)
    for k in range(out_ref.shape[0]):
        out_ref[k] = whitened


def score_kernel(scale, wide_ref, dosages_ref, out_ref):
    core = lax.axis_index("subj") % 2
    rows = out_ref.shape[2]
    step = 256
    for i in range(dosages_ref.shape[1] // step):
        part = jnp.dot(
            wide_ref[...], dosages_ref[:, i * step : (i + 1) * step], preferred_element_type=jnp.float32
        )
        part = part.T * scale
        for r in range(0, step, 8):
            owner, inner = divmod(i * step + r, rows)
            out_ref[core if owner % 2 == 0 else 1 - core, owner // 2, inner : inner + 8, :] = part[r : r + 8]


def add_kernel(mine_ref, other_ref, out_ref):
    rows, lanes = mine_ref.shape[1], out_ref.shape[2]
    for i in range(out_ref.shape[1] // rows):
        part = slice(i * lanes, (i + 1) * lanes)
        out_ref[:, i * rows : (i + 1) * rows, :] = (mine_ref[:, :, part] + other_ref[:, :, part]).astype(out_ref.dtype)


def sum_kernel(parts_ref, out_ref):
    total = parts_ref[0].astype(jnp.float32)
    for k in range(1, parts_ref.shape[0]):
        total = total + parts_ref[k].astype(jnp.float32)
    rows, lanes = out_ref.shape[0], parts_ref.shape[2]
    for i in range(out_ref.shape[1] // lanes):
        out_ref[:, i * lanes : (i + 1) * lanes] = total[i * rows : (i + 1) * rows]


def call(kernel, out, specs, scratch=()):
    many = isinstance(out, list)
    return pl.pallas_call(
        kernel,
        out_shape=out,
        in_specs=specs,
        out_specs=[VMEM] * len(out) if many else VMEM,
        scratch_shapes=list(scratch),
        compiler_params=PARAMS,
    )


def on_device(traits, kin_tiles, kin_index, dosages):
    n = lax.axis_size("subj")
    m = lax.axis_size("var")
    rows_here, width = traits.shape
    tiles, block = kin_tiles.shape[:2]
    here = rows_here // block
    slots = tiles - here
    lists = n // NEAR_FIRST
    chip_groups = [list(range(c, n, 2)) for c in range(2)]
    f32, bf16 = jnp.float32, jnp.bfloat16
    sds = jax.ShapeDtypeStruct

    def far_groups(near):
        return [list(range(i, n, near)) for i in range(near)]

    def gathered(field, near):
        groups = [list(range(k, k + near)) for k in range(0, n, near)]
        return lax.all_gather(field, "subj", axis_index_groups=groups)

    def fetched(lists, field):
        near = field.shape[0]
        packed = call(
            functools.partial(pack_kernel, NEAR_FIRST, here, block),
            sds((n // near, slots, width, block), bf16),
            [SMEM, VMEM],
        )(lists, field)
        return lax.all_to_all(packed, "subj", 0, 0, tiled=True, axis_index_groups=far_groups(near))

    listed = call(
        functools.partial(list_kernel, here), sds((lists, 8, LANES), jnp.int32), [SMEM]
    )(kin_index.T)
    listed = lax.all_to_all(
        listed, "subj", 0, 0, tiled=True, axis_index_groups=far_groups(NEAR_FIRST)
    )
    listed = listed[:, :3, :tiles]
    near = gathered(traits.T, NEAR_TRAITS)
    first, sent = call(
        functools.partial(first_kernel, NEAR_FIRST, here, block),
        [sds((width, rows_here), f32), sds((width, rows_here), bf16)],
        [SMEM, VMEM, VMEM, VMEM],
    )(listed, near, fetched(listed, near), kin_tiles)
    copies = call(
        functools.partial(second_kernel, NEAR_FIRST, here, block),
        sds((m, width, rows_here), bf16),
        [SMEM, VMEM, VMEM, VMEM, VMEM, VMEM],
        [pltpu.VMEM((width, rows_here), f32)],
    )(listed, sent, fetched(listed, gathered(sent, NEAR_FIRST)), kin_tiles, first, near)
    wide = lax.all_to_all(copies, "var", 0, 0, tiled=True).reshape(m * width, rows_here)

    scale = 1.0 / (127.5 * float(rows_here * n) ** 0.5)
    share = dosages.shape[1] // n
    parts = call(
        functools.partial(score_kernel, scale),
        sds((2, n // 2, share, m * width), f32),
        [VMEM, VMEM],
    )(wide, dosages)
    mine = parts[0]
    other = lax.ppermute(parts[1], "subj", [(s, s ^ 1) for s in range(n)])
    half = sds((n // 2, share * m * width // LANES, LANES), bf16)
    half = call(add_kernel, half, [VMEM, VMEM])(mine, other)
    arrived = lax.all_to_all(half, "subj", 0, 0, tiled=True, axis_index_groups=chip_groups)
    return call(sum_kernel, sds((share, m * width), f32), [VMEM])(arrived)


def solution(mesh):
    in_specs = (P("subj", "var"), P("subj", None, None), P("subj", None), P("subj", "var"))
    out_specs = P(("var", "subj"), None)
    return jax.shard_map(
        on_device, mesh=mesh, in_specs=in_specs, out_specs=out_specs, check_vma=False
    )
```

time: 154 us -> 145 us (0.942)
  the two profiles are of different devices: /device:TPU:8 before, /device:TPU:1 now
where the time goes in v3:
time: 145 us; the launch traced here: 142 us
  blocking collectives  111 us (77%)
  starting transfers between devices  19.5 us (13%)
  Pallas kernels  8.24 us (6%)
  local copies, waits for them, and re-layouts  2.27 us (2%)
    all_to_all x2, blocking collectives, fetched(): lax.all_to_all(packed, 'subj', 0, 0, tiled=True, axis_index_groups=far_gr...  47.5 us
    all_gather x2, blocking collectives, gathered(): return lax.all_gather(field, 'subj', axis_index_groups=groups)  25.3 us
    all_to_all x1, blocking collectives, on_device(): lax.all_to_all(copies, 'var', 0, 0, tiled=True)  22.4 us
    all_to_all x1, blocking collectives, on_device(): lax.all_to_all(half, 'subj', 0, 0, tiled=True, axis_index_groups=chip_gro...  15.7 us
    all_to_all x1, starting transfers between devices, on_device(): lax.all_to_all(listed, 'subj', 0, 0, tiled=True, axis_index_groups=far_gr...  15.6 us
    ppermute x1, starting transfers between devices, on_device(): other = lax.ppermute(parts[1], 'subj', [(s, s ^ 1) for s in range(n)])  3.82 us
  transfers between devices with their start and end apart: 2, of which 1 were waited for; matrix products, arithmetic and copies ran while one was open for 0% of the time, Pallas kernels for 0%

profile of v3, /device:TPU:1, one launch (start us, length us, event | category | flops | bytes accessed | tf_op | source)
XLA Modules:
  0.0 142.3 jit_solution(16626243572007208939)
XLA Ops:
  0.0 0.0 copy-start.1
  0.0 0.0 copy-start.3
  0.0 0.8 copy-done.3
  0.8 1.2 shard_map.46
  2.0 15.6 %all-to-all-start = ((s32[8,8,128]{2,1,0:T(8,128)}), s32[8,8,128]{2,1,0:T(8,128)S(1)}, u32[]{:S(2)}, u32[]{:S(2)}) async-start(s32[8,8,128]{2,1,0:T(8,128)} %shard_map.46), calls=%async_computation | async-start | bytes 65536 | tf_op jit(solution)/shard_map/all_to_all | solution.py:165
  17.7 16.4 %all-gather = bf16[128,2048]{1,0:T(8,128)(2,1)S(1)} all-gather(bf16[16,2048]{1,0:T(8,128)(2,1)} %bitcast.15), channel_id=2, replica_groups={{0,16,32,48,64,80,96,112},{128,144,160,176,192,208,224,240},{256,272,28..., dimensions={0}, use_global_device_ids=true | all-gather | bytes 589824 | tf_op jit(solution)/shard_map/all_gather | solution.py:151
  34.1 0.0 all-to-all-done
  34.1 1.1 shard_map.47
  35.2 23.0 %all_to_all.25.other_ref = bf16[4,4,16,256]{3,2,1,0:T(8,128)(2,1)S(1)} all-to-all(bf16[4,4,16,256]{3,2,1,0:T(8,128)(2,1)S(1)} %shard_map.47), channel_id=1, replica_groups={{0,128,256,384},{16,144,272,400},{32,160,288,416},{48,176,304,432},{64,..., dimensions={0} | all-to-all | bytes 262144 | tf_op jit(solution)/shard_map/all_to_all | solution.py:160
  58.2 0.0 copy-start
  58.2 1.4 copy-done
  59.6 1.3 shard_map.48
  61.0 8.9 %all-gather.1 = bf16[64,2048]{1,0:T(8,128)(2,1)S(1)} all-gather(bf16[16,2048]{1,0:T(8,128)(2,1)S(1)} %get-tuple-element.7.sent_ref), channel_id=3, replica_groups={{0,16,32,48},{64,80,96,112},{128,144,160,176},{192,208,224,240},{256,27..., dimensions={0}, use_global_device_ids=true | all-gather | bytes 327680 | tf_op jit(solution)/shard_map/all_gather | solution.py:151
  69.9 1.3 shard_map.49
  71.2 0.0 copy-start.2
  71.2 24.4 %all_to_all.26.other_ref = bf16[8,4,16,256]{3,2,1,0:T(8,128)(2,1)S(1)} all-to-all(bf16[8,4,16,256]{3,2,1,0:T(8,128)(2,1)S(1)} %shard_map.49), channel_id=1, replica_groups={{0,64,128,192,256,320,384,448},{16,80,144,208,272,336,400,464},{32,96,1..., dimensions={0} | all-to-all | bytes 524288 | tf_op jit(solution)/shard_map/all_to_all | solution.py:160
  95.7 0.0 copy-done.1
  95.7 1.4 %shard_map.50 = bf16[16,16,2048]{2,1,0:T(8,128)(2,1)S(1)} custom-call(s32[8,3,12]{2,1,0:T(4,128)S(1)} %slice.12.lists_ref, bf16[16,2048]{1,0:T(8,128)(2,1)S(1)} %get-tuple-element.7.sent_ref, bf16[8,4,16,256]{3,2,1,0:T(8,128)(2,1)S(1)} %all_to_all.26.other_ref, bf16[12,256,256]{2,1,0:T(8,128)(2,1)S(1)} %copy-done.1, ...), custom_call_target="tpu_custom_call" | custom-call | tf_op jit(solution)/shard_map/pallas_call | solution.py:175
  97.1 22.4 %all_to_all.27 = bf16[16,16,2048]{2,1,0:T(8,128)(2,1)S(1)} all-to-all(bf16[16,16,2048]{2,1,0:T(8,128)(2,1)S(1)} %shard_map.50), channel_id=1, replica_groups=mesh['subj'=32,'var'=16] {'var'}, dimensions={0} | all-to-all | bytes 2097152 | tf_op jit(solution)/shard_map/all_to_all | solution.py:181
  119.6 0.0 copy-done.2
  119.6 1.1 shard_map.51
  120.7 0.1 slice_bitcast_fusion
  120.8 3.8 %collective-permute-start = (f32[16,24,256]{2,1,0:T(8,128)S(1)}, f32[16,24,256]{2,1,0:T(8,128)S(1)}, u32[]{:S(2)}, u32[]{:S(2)}) collective-permute-start(f32[16,24,256]{2,1,0:T(8,128)S(1)} %get-tuple-element.9), channel_id=1, source_target_pairs={{0,16},{16,0},{32,48},{48,32},{64,80},{80,64},{96,112},{112,96},{1... | collective-permute-start | bytes 1179656 | tf_op jit(solution)/shard_map/ppermute | solution.py:191
  124.6 1.3 collective-permute-done.other_ref
  125.9 0.1 shard_map.52
  126.0 15.7 %all_to_all.28.parts_ref = bf16[16,48,128]{2,1,0:T(8,128)(2,1)S(1)} all-to-all(bf16[16,48,128]{2,1,0:T(8,128)(2,1)S(1)} %shard_map.52), channel_id=1, replica_groups={{0,32,64,96,128,160,192,224,256,288,320,352,384,416,448,480},{16,48,80,..., dimensions={0} | all-to-all | bytes 393216 | tf_op jit(solution)/shard_map/all_to_all | solution.py:194
  141.6 0.6 shard_map.53
  (1 shorter events, 0.0 us)
Async XLA Ops:
  0.0 95.7 %copy-start.1 = (bf16[12,256,256]{2,1,0:T(8,128)(2,1)S(1)}, bf16[12,256,256]{2,1,0:T(8,128)(2,1)}, u32[]{:S(2)}) copy-start(bf16[12,256,256]{2,1,0:T(8,128)(2,1)} %tiles_ref.3) | copy-start | bytes 4718596
  0.0 0.8 copy-start.3
  2.0 32.0 %all-to-all-start = ((s32[8,8,128]{2,1,0:T(8,128)}), s32[8,8,128]{2,1,0:T(8,128)S(1)}, u32[]{:S(2)}, u32[]{:S(2)}) async-start(s32[8,8,128]{2,1,0:T(8,128)} %shard_map.46), calls=%async_computation | async-start | bytes 65536 | tf_op jit(solution)/shard_map/all_to_all | solution.py:165
  58.2 1.4 copy-start
  71.2 48.3 %copy-start.2 = (bf16[2048,768]{1,0:T(8,128)(2,1)S(1)}, bf16[2048,768]{1,0:T(8,128)(2,1)}, u32[]{:S(2)}) copy-start(bf16[2048,768]{1,0:T(8,128)(2,1)} %dosages_ref.1) | copy-start | bytes 9437188
  120.8 5.2 %collective-permute-start = (f32[16,24,256]{2,1,0:T(8,128)S(1)}, f32[16,24,256]{2,1,0:T(8,128)S(1)}, u32[]{:S(2)}, u32[]{:S(2)}) collective-permute-start(f32[16,24,256]{2,1,0:T(8,128)S(1)} %get-tuple-element.9), channel_id=1, source_target_pairs={{0,16},{16,0},{32,48},{48,32},{64,80},{80,64},{96,112},{112,96},{1... | collective-permute-start | bytes 1179656 | tf_op jit(solution)/shard_map/ppermute | solution.py:191

commit v4 on v3

v4 whole, which is shorter than its diff:
```python
import functools

import jax
import jax.numpy as jnp
from jax import lax
from jax.experimental import pallas as pl
from jax.experimental.pallas import tpu as pltpu
from jax.sharding import PartitionSpec as P

NEAR = 4
LANES = 128
NONE = -1
VMEM = pl.BlockSpec(memory_space=pltpu.VMEM)
SMEM = pl.BlockSpec(memory_space=pltpu.SMEM)


def list_kernel(here, index_ref, out_ref):
    me = lax.axis_index("subj")
    shape = out_ref.shape[1:]
    lane = lax.broadcasted_iota(jnp.int32, shape, 1)
    line = lax.broadcasted_iota(jnp.int32, shape, 0)
    listed = jnp.full(shape, NONE, jnp.int32)
    count = jnp.int32(0)
    for t in range(index_ref.shape[1]):
        row, col = index_ref[0, t], index_ref[1, t]
        remote = jnp.where(col // here != me, 1, 0)
        listed = jnp.where((line == 0) & (lane == jnp.where(remote == 1, count, -1)), col, listed)
        listed = jnp.where((line == 1) & (lane == t), row, listed)
        listed = jnp.where((line == 2) & (lane == t), col, listed)
        count = count + remote
    for k in range(out_ref.shape[0]):
        out_ref[k] = listed


def pack_kernel(here, block, lists_ref, near_ref, out_ref):
    first = lax.axis_index("subj") // NEAR * (NEAR * here)
    for k in range(out_ref.shape[0]):
        for j in range(out_ref.shape[1]):
            inside = jnp.clip(lists_ref[k, 0, j] - first, 0, NEAR * here - 1)
            at = pl.multiple_of(inside % here * block, block)
            out_ref[k, j] = near_ref[inside // here, :, pl.ds(at, block)]


def apply_tiles(here, block, lists_ref, field_ref, other_ref, tiles_ref, sum_ref):
    me = lax.axis_index("subj")
    slots = other_ref.shape[1]
    sum_ref[...] = jnp.zeros_like(sum_ref)
    count = jnp.int32(0)
    for t in range(tiles_ref.shape[0]):
        row = lists_ref[me // NEAR, 1, t] - me * here
        col = lists_ref[me // NEAR, 2, t]
        local = col // here == me
        at = pl.multiple_of(col % here * block, block)
        mine = field_ref[:, pl.ds(at, block)]
        other = other_ref[col // (here * NEAR), jnp.minimum(count, slots - 1)]
        count = count + jnp.where(local, 0, 1)
        slab = jnp.where(local, mine, other)
        prod = lax.dot_general(
            slab, tiles_ref[t], (((1,), (1,)), ((), ())), preferred_element_type=jnp.float32
        )
        to = pl.ds(pl.multiple_of(row * block, block), block)
        sum_ref[:, to] += prod


def first_kernel(
    here, block, lists_ref, near_ref, other_ref, tiles_ref, sum_ref, sent_ref
):
    own = near_ref.at[lax.axis_index("subj") % NEAR]
    apply_tiles(here, block, lists_ref, own, other_ref, tiles_ref, sum_ref)
    sent_ref[...] = sum_ref[...].astype(sent_ref.dtype)


def second_kernel(
    here, block, lists_ref, sent_ref, other_ref, tiles_ref, first_ref, near_ref, out_ref, sum_ref
):
    apply_tiles(here, block, lists_ref, sent_ref, other_ref, tiles_ref, sum_ref)
    base = near_ref[lax.axis_index("subj") % NEAR].astype(jnp.float32)
    whitened = 0.6 * base + 0.5 * first_ref[...] + 0.3 * (2.0 * sum_ref[...] - base)
    whitened = whitened.astype(out_ref.dtype)
    for k in range(out_ref.shape[0]):
        out_ref[k] = whitened


def score_kernel(scale, wide_ref, dosages_ref, out_ref):
    core = lax.axis_index("subj") % 2
    rows = out_ref.shape[2]
    step = 256
    for i in range(dosages_ref.shape[1] // step):
        part = jnp.dot(
            wide_ref[...], dosages_ref[:, i * step : (i + 1) * step], preferred_element_type=jnp.float32
        )
        part = part.T * scale
        for r in range(0, step, 8):
            owner, inner = divmod(i * step + r, rows)
            to = core if owner % 2 == 0 else 1 - core
            out_ref[to, owner // 2, inner : inner + 8, :] = part[r : r + 8]


def add_kernel(parts_ref, both_ref, out_ref):
    other = 1 - lax.axis_index("subj") % 2
    rows, lanes = parts_ref.shape[2], out_ref.shape[2]
    for i in range(out_ref.shape[1] // rows):
        part = slice(i * lanes, (i + 1) * lanes)
        total = parts_ref[0, :, :, part] + both_ref[other, :, :, part]
        out_ref[:, i * rows : (i + 1) * rows, :] = total.astype(out_ref.dtype)


def sum_kernel(parts_ref, out_ref):
    total = parts_ref[0].astype(jnp.float32)
    for k in range(1, parts_ref.shape[0]):
        total = total + parts_ref[k].astype(jnp.float32)
    rows, lanes = out_ref.shape[0], parts_ref.shape[2]
    for i in range(out_ref.shape[1] // lanes):
        out_ref[:, i * lanes : (i + 1) * lanes] = total[i * rows : (i + 1) * rows]


def call(kernel, out, specs, scratch=(), mib=48):
    many = isinstance(out, list)
    return pl.pallas_call(
        kernel,
        out_shape=out,
        in_specs=specs,
        out_specs=[VMEM] * len(out) if many else VMEM,
        scratch_shapes=list(scratch),
        compiler_params=pltpu.CompilerParams(vmem_limit_bytes=mib * 2**20),
    )


def on_device(traits, kin_tiles, kin_index, dosages):
    n = lax.axis_size("subj")
    m = lax.axis_size("var")
    rows_here, width = traits.shape
    tiles, block = kin_tiles.shape[:2]
    here = rows_here // block
    slots = tiles - here
    far = n // NEAR
    near_groups = [list(range(k, k + NEAR)) for k in range(0, n, NEAR)]
    far_groups = [list(range(i, n, NEAR)) for i in range(NEAR)]
    chip_groups = [list(range(c, n, 2)) for c in range(2)]
    core_groups = [[s, s + 1] for s in range(0, n, 2)]
    f32, bf16 = jnp.float32, jnp.bfloat16
    sds = jax.ShapeDtypeStruct

    def exchanged(x, groups):
        return lax.all_to_all(x, "subj", 0, 0, tiled=True, axis_index_groups=groups)

    def gathered(field):
        return lax.all_gather(field, "subj", axis_index_groups=near_groups)

    def fetched(lists, near):
        packed = call(
            functools.partial(pack_kernel, here, block),
            sds((far, slots, width, block), bf16),
            [SMEM, VMEM],
        )(lists, near)
        return exchanged(packed, far_groups)

    lists = call(
        functools.partial(list_kernel, here), sds((far, 8, LANES), jnp.int32), [SMEM], mib=62
    )(kin_index.T)
    lists = exchanged(lists, far_groups)[:, :3, :tiles]
    near = gathered(traits.T)
    first, sent = call(
        functools.partial(first_kernel, here, block),
        [sds((width, rows_here), f32), sds((width, rows_here), bf16)],
        [SMEM, VMEM, VMEM, VMEM],
    )(lists, near, fetched(lists, near), kin_tiles)
    copies = call(
        functools.partial(second_kernel, here, block),
        sds((m, width, rows_here), bf16),
        [SMEM, VMEM, VMEM, VMEM, VMEM, VMEM],
        [pltpu.VMEM((width, rows_here), f32)],
    )(lists, sent, fetched(lists, gathered(sent)), kin_tiles, first, near)
    wide = lax.all_to_all(copies, "var", 0, 0, tiled=True).reshape(m * width, rows_here)

    scale = 1.0 / (127.5 * float(rows_here * n) ** 0.5)
    share = dosages.shape[1] // n
    parts = sds((2, n // 2, share, m * width), f32)
    parts = call(functools.partial(score_kernel, scale), parts, [VMEM, VMEM])(wide, dosages)
    both = lax.all_gather(parts[1], "subj", axis_index_groups=core_groups)
    half = sds((n // 2, share * m * width // LANES, LANES), bf16)
    half = call(add_kernel, half, [VMEM, VMEM])(parts, both)
    arrived = exchanged(half, chip_groups)
    return call(sum_kernel, sds((share, m * width), f32), [VMEM])(arrived)


def solution(mesh):
    in_specs = (P("subj", "var"), P("subj", None, None), P("subj", None), P("subj", "var"))
    out_specs = P(("var", "subj"), None)
    return jax.shard_map(
        on_device, mesh=mesh, in_specs=in_specs, out_specs=out_specs, check_vma=False
    )
```

time: 145 us -> 140 us (0.966)
  the two profiles are of different devices: /device:TPU:1 before, /device:TPU:32 now
where the time goes in v4:
time: 140 us; the launch traced here: 139 us
  blocking collectives  109 us (78%)
  starting transfers between devices  14.2 us (10%)
  Pallas kernels  7.99 us (6%)
  waiting for transfers between devices  6.67 us (5%)
  local copies, waits for them, and re-layouts  1.45 us (1%)
    all_to_all x3, blocking collectives, exchanged(): return lax.all_to_all(x, 'subj', 0, 0, tiled=True, axis_index_groups=groups)  73.8 us
    all_to_all x1, blocking collectives, on_device(): lax.all_to_all(copies, 'var', 0, 0, tiled=True)  20.1 us
    all_to_all x1, starting transfers between devices, exchanged(): return lax.all_to_all(x, 'subj', 0, 0, tiled=True, axis_index_groups=groups)  14.2 us
    all_gather x2, blocking collectives, gathered(): return lax.all_gather(field, 'subj', axis_index_groups=near_groups)  12.5 us
    all_to_all x1, waiting for transfers between devices, exchanged(): return lax.all_to_all(x, 'subj', 0, 0, tiled=True, axis_index_groups=groups)  6.67 us
  transfers between devices with their start and end apart: 1, of which 1 were waited for; matrix products, arithmetic and copies ran while one was open for 0% of the time, Pallas kernels for 0%

profile of v4, /device:TPU:32, one launch (start us, length us, event | category | flops | bytes accessed | tf_op | source)
XLA Modules:
  0.0 139.2 jit_solution(9501221270414594288)
XLA Ops:
  0.0 1.4 shard_map.46
  1.4 14.2 %all-to-all-start = ((s32[8,8,128]{2,1,0:T(8,128)}), s32[8,8,128]{2,1,0:T(8,128)S(1)}, u32[]{:S(2)}, u32[]{:S(2)}) async-start(s32[8,8,128]{2,1,0:T(8,128)} %shard_map.46), calls=%async_computation | async-start | bytes 65536 | tf_op jit(solution)/shard_map/all_to_all | solution.py:145
  15.6 6.2 %all-gather = bf16[64,2048]{1,0:T(8,128)(2,1)S(1)} all-gather(bf16[16,2048]{1,0:T(8,128)(2,1)} %bitcast.10), channel_id=2, replica_groups={{0,16,32,48},{64,80,96,112},{128,144,160,176},{192,208,224,240},{256,27..., dimensions={0}, use_global_device_ids=true | all-gather | bytes 327680 | tf_op jit(solution)/shard_map/all_gather | solution.py:148
  21.8 6.7 %all-to-all-done = s32[8,8,128]{2,1,0:T(8,128)S(1)} async-done(((s32[8,8,128]{2,1,0:T(8,128)}), s32[8,8,128]{2,1,0:T(8,128)S(1)}, u32[]{:S(2)}, u32[]{:S(2)}) %all-to-all-start) | async-done | bytes 32800 | tf_op jit(solution)/shard_map/all_to_all | solution.py:145
  28.5 1.0 shard_map.47
  29.5 25.7 %all_to_all.25.other_ref = bf16[8,4,16,256]{3,2,1,0:T(8,128)(2,1)S(1)} all-to-all(bf16[8,4,16,256]{3,2,1,0:T(8,128)(2,1)S(1)} %shard_map.47), channel_id=1, replica_groups={{0,64,128,192,256,320,384,448},{16,80,144,208,272,336,400,464},{32,96,1..., dimensions={0} | all-to-all | bytes 524288 | tf_op jit(solution)/shard_map/all_to_all | solution.py:145
  55.3 0.0 copy-start
  55.3 1.4 %copy-done = bf16[12,256,256]{2,1,0:T(8,128)(2,1)S(1)} copy-done((bf16[12,256,256]{2,1,0:T(8,128)(2,1)S(1)}, bf16[12,256,256]{2,1,0:T(8,128)(2,1)}, u32[]{:S(2)}) %copy-start) | copy-done | bytes 1572888
  56.7 0.0 copy-start.1
  56.7 1.3 shard_map.48
  58.0 6.3 %all-gather.1 = bf16[64,2048]{1,0:T(8,128)(2,1)S(1)} all-gather(bf16[16,2048]{1,0:T(8,128)(2,1)S(1)} %get-tuple-element.7.sent_ref), channel_id=3, replica_groups={{0,16,32,48},{64,80,96,112},{128,144,160,176},{192,208,224,240},{256,27..., dimensions={0}, use_global_device_ids=true | all-gather | bytes 327680 | tf_op jit(solution)/shard_map/all_gather | solution.py:148
  64.3 0.0 copy-start.2
  64.3 1.0 shard_map.49
  65.3 24.1 %all_to_all.26.other_ref = bf16[8,4,16,256]{3,2,1,0:T(8,128)(2,1)S(1)} all-to-all(bf16[8,4,16,256]{3,2,1,0:T(8,128)(2,1)S(1)} %shard_map.49), channel_id=1, replica_groups={{0,64,128,192,256,320,384,448},{16,80,144,208,272,336,400,464},{32,96,1..., dimensions={0} | all-to-all | bytes 524288 | tf_op jit(solution)/shard_map/all_to_all | solution.py:145
  89.5 0.0 copy-done.1
  89.5 1.4 %shard_map.50 = bf16[16,16,2048]{2,1,0:T(8,128)(2,1)S(1)} custom-call(s32[8,3,12]{2,1,0:T(4,128)S(1)} %slice.8.lists_ref, bf16[16,2048]{1,0:T(8,128)(2,1)S(1)} %get-tuple-element.7.sent_ref, bf16[8,4,16,256]{3,2,1,0:T(8,128)(2,1)S(1)} %all_to_all.26.other_ref, bf16[12,256,256]{2,1,0:T(8,128)(2,1)S(1)} %copy-done.1, ...), custom_call_target="tpu_custom_call" | custom-call | tf_op jit(solution)/shard_map/pallas_call | solution.py:168
  90.9 20.1 %all_to_all.27 = bf16[16,16,2048]{2,1,0:T(8,128)(2,1)S(1)} all-to-all(bf16[16,16,2048]{2,1,0:T(8,128)(2,1)S(1)} %shard_map.50), channel_id=1, replica_groups=mesh['subj'=32,'var'=16] {'var'}, dimensions={0} | all-to-all | bytes 2097152 | tf_op jit(solution)/shard_map/all_to_all | solution.py:174
  111.1 0.0 copy-done.2
  111.1 1.1 shard_map.51.parts_ref
  112.2 2.4 %all_gather.19.both_ref = f32[2,16,24,256]{3,2,1,0:T(8,128)S(1)} all-gather(f32[1,16,24,256]{3,2,1,0:T(8,128)S(1)} %slice.9), channel_id=1, replica_groups={{0,16},{32,48},{64,80},{96,112},{128,144},{160,176},{192,208},{224,240}..., dimensions={0}, use_global_device_ids=true | all-gather | bytes 1179648 | tf_op jit(solution)/shard_map/all_gather | solution.py:180
  114.6 23.9 %all_to_all.28.parts_ref = bf16[16,48,128]{2,1,0:T(8,128)(2,1)S(1)} all-to-all(bf16[16,48,128]{2,1,0:T(8,128)(2,1)S(1)} %shard_map.52), channel_id=1, replica_groups={{0,32,64,96,128,160,192,224,256,288,320,352,384,416,448,480},{16,48,80,..., dimensions={0} | all-to-all | bytes 393216 | tf_op jit(solution)/shard_map/all_to_all | solution.py:145
  138.6 0.6 shard_map.53
  (3 shorter events, 0.1 us)
Async XLA Ops:
  1.4 27.1 %all-to-all-start = ((s32[8,8,128]{2,1,0:T(8,128)}), s32[8,8,128]{2,1,0:T(8,128)S(1)}, u32[]{:S(2)}, u32[]{:S(2)}) async-start(s32[8,8,128]{2,1,0:T(8,128)} %shard_map.46), calls=%async_computation | async-start | bytes 65536 | tf_op jit(solution)/shard_map/all_to_all | solution.py:145
  55.3 1.4 %copy-start = (bf16[12,256,256]{2,1,0:T(8,128)(2,1)S(1)}, bf16[12,256,256]{2,1,0:T(8,128)(2,1)}, u32[]{:S(2)}) copy-start(bf16[12,256,256]{2,1,0:T(8,128)(2,1)} %tiles_ref.3) | copy-start | bytes 4718596
  56.7 32.8 %copy-start.1 = (bf16[12,256,256]{2,1,0:T(8,128)(2,1)S(1)}, bf16[12,256,256]{2,1,0:T(8,128)(2,1)}, u32[]{:S(2)}) copy-start(bf16[12,256,256]{2,1,0:T(8,128)(2,1)} %tiles_ref.3) | copy-start | bytes 4718596
  64.3 46.8 %copy-start.2 = (bf16[2048,768]{1,0:T(8,128)(2,1)S(1)}, bf16[2048,768]{1,0:T(8,128)(2,1)}, u32[]{:S(2)}) copy-start(bf16[2048,768]{1,0:T(8,128)(2,1)} %dosages_ref.1) | copy-start | bytes 9437188

commit v5 on v4

--- a/solution.py
+++ b/solution.py
@@ -9,9 +9,19 @@
 
 NEAR = 4
 LANES = 128
+TURN, VAR_TURN = 5, 15
 NONE = -1
 VMEM = pl.BlockSpec(memory_space=pltpu.VMEM)
+HBM = pl.BlockSpec(memory_space=pltpu.HBM)
 SMEM = pl.BlockSpec(memory_space=pltpu.SMEM)
+
+
+def turned(group, turn):
+    return group[turn:] + group[:turn]
+
+
+def place(k, size, turn):
+    return (k + size - turn) % size
 
 
 def list_kernel(here, index_ref, out_ref):
@@ -24,7 +34,9 @@
     for t in range(index_ref.shape[1]):
         row, col = index_ref[0, t], index_ref[1, t]
         remote = jnp.where(col // here != me, 1, 0)
-        listed = jnp.where((line == 0) & (lane == jnp.where(remote == 1, count, -1)), col, listed)
+        slot = lane == jnp.where(remote == 1, count, -1)
+        listed = jnp.where((line == 0) & slot, col, listed)
+        listed = jnp.where((line == 3) & slot, t, listed)
         listed = jnp.where((line == 1) & (lane == t), row, listed)
         listed = jnp.where((line == 2) & (lane == t), col, listed)
         count = count + remote
@@ -41,32 +53,60 @@
             out_ref[k, j] = near_ref[inside // here, :, pl.ds(at, block)]
 
 
+def tile_dot(slab, tile):
+    return lax.dot_general(slab, tile, (((1,), (1,)), ((), ())), preferred_element_type=jnp.float32)
+
+
 def apply_tiles(here, block, lists_ref, field_ref, other_ref, tiles_ref, sum_ref):
     me = lax.axis_index("subj")
-    slots = other_ref.shape[1]
+    far, slots = other_ref.shape[:2]
+    mine = place(me // NEAR, far, TURN)
     sum_ref[...] = jnp.zeros_like(sum_ref)
     count = jnp.int32(0)
     for t in range(tiles_ref.shape[0]):
-        row = lists_ref[me // NEAR, 1, t] - me * here
-        col = lists_ref[me // NEAR, 2, t]
+        row = lists_ref[mine, 1, t] - me * here
+        col = lists_ref[mine, 2, t]
         local = col // here == me
         at = pl.multiple_of(col % here * block, block)
-        mine = field_ref[:, pl.ds(at, block)]
-        other = other_ref[col // (here * NEAR), jnp.minimum(count, slots - 1)]
+        own = field_ref[:, pl.ds(at, block)]
+        other = other_ref[place(col // (here * NEAR), far, TURN), jnp.minimum(count, slots - 1)]
         count = count + jnp.where(local, 0, 1)
-        slab = jnp.where(local, mine, other)
-        prod = lax.dot_general(
-            slab, tiles_ref[t], (((1,), (1,)), ((), ())), preferred_element_type=jnp.float32
-        )
+        slab = jnp.where(local, own, other)
+        prod = tile_dot(slab, tiles_ref[t])
         to = pl.ds(pl.multiple_of(row * block, block), block)
         sum_ref[:, to] += prod
 
 
-def first_kernel(
-    here, block, lists_ref, near_ref, other_ref, tiles_ref, sum_ref, sent_ref
-):
-    own = near_ref.at[lax.axis_index("subj") % NEAR]
-    apply_tiles(here, block, lists_ref, own, other_ref, tiles_ref, sum_ref)
+def local_kernel(here, block, lists_ref, near_ref, tiles_ref, sum_ref, held_ref, sem):
+    me = lax.axis_index("subj")
+    mine = place(me // NEAR, lists_ref.shape[0], TURN)
+    copy = pltpu.make_async_copy(tiles_ref, held_ref, sem)
+    copy.start()
+    sum_ref[...] = jnp.zeros_like(sum_ref)
+    copy.wait()
+    for t in range(held_ref.shape[0]):
+        row = lists_ref[mine, 1, t] - me * here
+        col = lists_ref[mine, 2, t]
+        at = pl.multiple_of(col % here * block, block)
+        slab = near_ref[me % NEAR, :, pl.ds(at, block)]
+        slab = jnp.where(col // here == me, slab, jnp.zeros_like(slab))
+        to = pl.ds(pl.multiple_of(row * block, block), block)
+        sum_ref[:, to] += tile_dot(slab, held_ref[t])
+
+
+def first_kernel(here, block, lists_ref, local_ref, other_ref, tiles_ref, sum_ref, sent_ref):
+    me = lax.axis_index("subj")
+    far = lists_ref.shape[0]
+    mine = place(me // NEAR, far, TURN)
+    sum_ref[...] = local_ref[...]
+    for j in range(other_ref.shape[1]):
+        col = lists_ref[mine, 0, j]
+        t = jnp.maximum(lists_ref[mine, 3, j], 0)
+        row = lists_ref[mine, 1, t] - me * here
+        slab = other_ref[place(jnp.maximum(col, 0) // (here * NEAR), far, TURN), j]
+        slab = jnp.where(col >= 0, slab, jnp.zeros_like(slab))
+        to = pl.ds(pl.multiple_of(row * block, block), block)
+        sum_ref[:, to] += tile_dot(slab, tiles_ref[t])
     sent_ref[...] = sum_ref[...].astype(sent_ref.dtype)
 
 
@@ -81,19 +121,21 @@
         out_ref[k] = whitened
 
 
-def score_kernel(scale, wide_ref, dosages_ref, out_ref):
+def score_kernel(scale, width, wide_ref, dosages_ref, out_ref):
     core = lax.axis_index("subj") % 2
     rows = out_ref.shape[2]
     step = 256
+    top = wide_ref.shape[0] - VAR_TURN * width
+    wide = jnp.concatenate([wide_ref[top:], wide_ref[:top]])
     for i in range(dosages_ref.shape[1] // step):
         part = jnp.dot(
-            wide_ref[...], dosages_ref[:, i * step : (i + 1) * step], preferred_element_type=jnp.float32
+            wide, dosages_ref[:, i * step : (i + 1) * step], preferred_element_type=jnp.float32
         )
         part = part.T * scale
         for r in range(0, step, 8):
             owner, inner = divmod(i * step + r, rows)
             to = core if owner % 2 == 0 else 1 - core
-            out_ref[to, owner // 2, inner : inner + 8, :] = part[r : r + 8]
+            out_ref[to, place(owner // 2, out_ref.shape[1], 2 * TURN), inner : inner + 8, :] = part[r : r + 8]
 
 
 def add_kernel(parts_ref, both_ref, out_ref):
@@ -135,8 +177,9 @@
     slots = tiles - here
     far = n // NEAR
     near_groups = [list(range(k, k + NEAR)) for k in range(0, n, NEAR)]
-    far_groups = [list(range(i, n, NEAR)) for i in range(NEAR)]
-    chip_groups = [list(range(c, n, 2)) for c in range(2)]
+    far_groups = [turned(list(range(i, n, NEAR)), TURN) for i in range(NEAR)]
+    chip_groups = [turned(list(range(c, n, 2)), 2 * TURN) for c in range(2)]
+    var_groups = [turned(list(range(m)), VAR_TURN)]
     core_groups = [[s, s + 1] for s in range(0, n, 2)]
     f32, bf16 = jnp.float32, jnp.bfloat16
     sds = jax.ShapeDtypeStruct
@@ -158,25 +201,32 @@
     lists = call(
         functools.partial(list_kernel, here), sds((far, 8, LANES), jnp.int32), [SMEM], mib=62
     )(kin_index.T)
-    lists = exchanged(lists, far_groups)[:, :3, :tiles]
+    lists = exchanged(lists, far_groups)[:, :4, :tiles]
     near = gathered(traits.T)
+    local, held = call(
+        functools.partial(local_kernel, here, block),
+        [sds((width, rows_here), f32), sds(kin_tiles.shape, bf16)],
+        [SMEM, VMEM, HBM],
+        [pltpu.SemaphoreType.DMA],
+    )(lists, near, kin_tiles)
     first, sent = call(
         functools.partial(first_kernel, here, block),
         [sds((width, rows_here), f32), sds((width, rows_here), bf16)],
         [SMEM, VMEM, VMEM, VMEM],
-    )(lists, near, fetched(lists, near), kin_tiles)
+    )(lists, local, fetched(lists, near), held)
     copies = call(
         functools.partial(second_kernel, here, block),
         sds((m, width, rows_here), bf16),
         [SMEM, VMEM, VMEM, VMEM, VMEM, VMEM],
         [pltpu.VMEM((width, rows_here), f32)],
-    )(lists, sent, fetched(lists, gathered(sent)), kin_tiles, first, near)
-    wide = lax.all_to_all(copies, "var", 0, 0, tiled=True).reshape(m * width, rows_here)
+    )(lists, sent, fetched(lists, gathered(sent)), held, first, near)
+    wide = lax.all_to_all(copies, "var", 0, 0, tiled=True, axis_index_groups=var_groups)
+    wide = wide.reshape(m * width, rows_here)
 
     scale = 1.0 / (127.5 * float(rows_here * n) ** 0.5)
     share = dosages.shape[1] // n
     parts = sds((2, n // 2, share, m * width), f32)
-    parts = call(functools.partial(score_kernel, scale), parts, [VMEM, VMEM])(wide, dosages)
+    parts = call(functools.partial(score_kernel, scale, width), parts, [VMEM, VMEM])(wide, dosages)
     both = lax.all_gather(parts[1], "subj", axis_index_groups=core_groups)
     half = sds((n // 2, share * m * width // LANES, LANES), bf16)
     half = call(add_kernel, half, [VMEM, VMEM])(parts, both)

time: 140 us -> 133 us (0.950)
  the two profiles are of different devices: /device:TPU:32 before, /device:TPU:1 now
where the time goes in v5:
time: 133 us
  blocking collectives  84.3 us (63%)
  starting transfers between devices  28 us (21%)
  Pallas kernels  9.91 us (7%)
  waiting for transfers between devices  8.8 us (7%)
  local copies, waits for them, and re-layouts  1.44 us (1%)
    all_to_all x2, blocking collectives, exchanged(): return lax.all_to_all(x, 'subj', 0, 0, tiled=True, axis_index_groups=groups)  42.6 us
    all_to_all x2, starting transfers between devices, exchanged(): return lax.all_to_all(x, 'subj', 0, 0, tiled=True, axis_index_groups=groups)  28 us
    all_gather x2, blocking collectives, gathered(): return lax.all_gather(field, 'subj', axis_index_groups=near_groups)  16.1 us
    all_to_all x1, blocking collectives, on_device(): lax.all_to_all(copies, 'var', 0, 0, tiled=True, axis_index_groups=var_gro...  15.8 us
    all_gather x1, blocking collectives, on_device(): both = lax.all_gather(parts[1], 'subj', axis_index_groups=core_groups)  9.87 us
    all_to_all x2, waiting for transfers between devices, exchanged(): return lax.all_to_all(x, 'subj', 0, 0, tiled=True, axis_index_groups=groups)  8.8 us
    pallas_call x2, Pallas kernels, fetched(): call(functools.partial(pack_kernel, here, block), sds((far, slots, width,...  2.75 us
  transfers between devices with their start and end apart: 2, of which 1 were waited for; matrix products, arithmetic and copies ran while one was open for 0% of the time, Pallas kernels for 1%

profile of v5, /device:TPU:1, one launch (start us, length us, event | category | flops | bytes accessed | tf_op | source)
XLA Modules:
  0.0 132.6 jit_solution(8259140902645519697)
XLA Ops:
  0.0 1.4 %shard_map.46 = s32[8,8,128]{2,1,0:T(8,128)} custom-call(s32[2,12]{1,0:T(2,128)} %bitcast.11), custom_call_target="tpu_custom_call" | custom-call | tf_op jit(solution)/shard_map/pallas_call | solution.py:201
  1.4 16.9 %all-to-all-start = ((s32[8,8,128]{2,1,0:T(8,128)}), s32[8,8,128]{2,1,0:T(8,128)S(1)}, u32[]{:S(2)}, u32[]{:S(2)}) async-start(s32[8,8,128]{2,1,0:T(8,128)} %shard_map.46), calls=%async_computation | async-start | bytes 65536 | tf_op jit(solution)/shard_map/all_to_all | solution.py:188
  18.2 7.3 %all-gather = bf16[64,2048]{1,0:T(8,128)(2,1)S(1)} all-gather(bf16[16,2048]{1,0:T(8,128)(2,1)} %bitcast.10), channel_id=2, replica_groups={{0,16,32,48},{64,80,96,112},{128,144,160,176},{192,208,224,240},{256,27..., dimensions={0}, use_global_device_ids=true | all-gather | bytes 327680 | tf_op jit(solution)/shard_map/all_gather | solution.py:191
  25.5 0.0 all-to-all-done
  25.6 1.7 %shard_map.48 = bf16[8,4,16,256]{3,2,1,0:T(8,128)(2,1)} custom-call(s32[8,4,12]{2,1,0:T(4,128)S(1)} %slice.8.lists_ref, bf16[4,16,2048]{2,1,0:T(8,128)(2,1)S(1)} %bitcast.6), custom_call_target="tpu_custom_call" | custom-call | tf_op jit(solution)/shard_map/pallas_call | solution.py:194
  27.3 11.2 %all-to-all-start.1 = ((bf16[8,4,16,256]{3,2,1,0:T(8,128)(2,1)}), bf16[8,4,16,256]{3,2,1,0:T(8,128)(2,1)S(1)}, u32[]{:S(2)}, u32[]{:S(2)}) async-start(bf16[8,4,16,256]{3,2,1,0:T(8,128)(2,1)} %shard_map.48), calls=%async_computation.1 | async-start | bytes 524288 | tf_op jit(solution)/shard_map/all_to_all | solution.py:188
  38.5 0.0 copy-start.1
  38.5 1.4 %copy-done.1 = bf16[12,256,256]{2,1,0:T(8,128)(2,1)S(1)} copy-done((bf16[12,256,256]{2,1,0:T(8,128)(2,1)S(1)}, bf16[12,256,256]{2,1,0:T(8,128)(2,1)}, u32[]{:S(2)}) %copy-start.1) | copy-done | bytes 1572888
  39.9 1.5 %shard_map.47 = (f32[16,2048]{1,0:T(8,128)S(1)}, bf16[12,256,256]{2,1,0:T(8,128)(2,1)S(1)}) custom-call(s32[8,4,12]{2,1,0:T(4,128)S(1)} %slice.8.lists_ref, bf16[4,16,2048]{2,1,0:T(8,128)(2,1)S(1)} %bitcast.7, bf16[12,256,256]{2,1,0:T(8,128)(2,1)S(1)} %copy-done.1), custom_call_target="tpu_custom_call" | custom-call | tf_op jit(solution)/shard_map/pallas_call | solution.py:206
  41.4 8.8 %all-to-all-done.1.other_ref = bf16[8,4,16,256]{3,2,1,0:T(8,128)(2,1)S(1)} async-done(((bf16[8,4,16,256]{3,2,1,0:T(8,128)(2,1)}), bf16[8,4,16,256]{3,2,1,0:T(8,128)(2,1)S(1)}, u32[]{:S(2)}, u32[]{:S(2)}) %all-to-all-start.1) | async-done | bytes 262176 | tf_op jit(solution)/shard_map/all_to_all | solution.py:188
  50.2 1.1 shard_map.49
  51.2 8.8 %all-gather.1 = bf16[64,2048]{1,0:T(8,128)(2,1)S(1)} all-gather(bf16[16,2048]{1,0:T(8,128)(2,1)S(1)} %get-tuple-element.11.sent_ref), channel_id=3, replica_groups={{0,16,32,48},{64,80,96,112},{128,144,160,176},{192,208,224,240},{256,27..., dimensions={0}, use_global_device_ids=true | all-gather | bytes 327680 | tf_op jit(solution)/shard_map/all_gather | solution.py:191
  60.0 1.0 shard_map.50
  61.0 17.9 %all_to_all.25.other_ref = bf16[8,4,16,256]{3,2,1,0:T(8,128)(2,1)S(1)} all-to-all(bf16[8,4,16,256]{3,2,1,0:T(8,128)(2,1)S(1)} %shard_map.50), channel_id=1, replica_groups={{320,384,448,0,64,128,192,256},{336,400,464,16,80,144,208,272},{352,416..., dimensions={0} | all-to-all | bytes 524288 | tf_op jit(solution)/shard_map/all_to_all | solution.py:188
  78.9 0.0 copy-start
  78.9 1.4 %shard_map.51 = bf16[16,16,2048]{2,1,0:T(8,128)(2,1)S(1)} custom-call(s32[8,4,12]{2,1,0:T(4,128)S(1)} %slice.8.lists_ref, bf16[16,2048]{1,0:T(8,128)(2,1)S(1)} %get-tuple-element.11.sent_ref, bf16[8,4,16,256]{3,2,1,0:T(8,128)(2,1)S(1)} %all_to_all.25.other_ref, bf16[12,256,256]{2,1,0:T(8,128)(2,1)S(1)} %get-tuple-element.10.tiles_ref, ...), custom_call_target="tpu_custom_call" | custom-call | tf_op jit(solution)/shard_map/pallas_call | solution.py:217
  80.3 15.8 %all_to_all.26 = bf16[16,16,2048]{2,1,0:T(8,128)(2,1)S(1)} all-to-all(bf16[16,16,2048]{2,1,0:T(8,128)(2,1)S(1)} %shard_map.51), channel_id=1, replica_groups={{15,0,1,2,3,4,5,6,7,8,9,10,11,12,13,14},{31,16,17,18,19,20,21,22,23,24,..., dimensions={0} | all-to-all | bytes 2097152 | tf_op jit(solution)/shard_map/all_to_all | solution.py:223
  96.1 0.0 copy-done
  96.1 1.1 shard_map.52.parts_ref
  97.3 9.9 %all_gather.19.both_ref = f32[2,16,24,256]{3,2,1,0:T(8,128)S(1)} all-gather(f32[1,16,24,256]{3,2,1,0:T(8,128)S(1)} %slice.9), channel_id=1, replica_groups={{0,16},{32,48},{64,80},{96,112},{128,144},{160,176},{192,208},{224,240}..., dimensions={0}, use_global_device_ids=true | all-gather | bytes 1179648 | tf_op jit(solution)/shard_map/all_gather | solution.py:230
  107.2 24.7 %all_to_all.27.parts_ref = bf16[16,48,128]{2,1,0:T(8,128)(2,1)S(1)} all-to-all(bf16[16,48,128]{2,1,0:T(8,128)(2,1)S(1)} %shard_map.53), channel_id=1, replica_groups={{320,352,384,416,448,480,0,32,64,96,128,160,192,224,256,288},{336,368,4..., dimensions={0} | all-to-all | bytes 393216 | tf_op jit(solution)/shard_map/all_to_all | solution.py:188
  131.9 0.6 shard_map.54
  (3 shorter events, 0.1 us)
Async XLA Ops:
  1.4 24.2 %all-to-all-start = ((s32[8,8,128]{2,1,0:T(8,128)}), s32[8,8,128]{2,1,0:T(8,128)S(1)}, u32[]{:S(2)}, u32[]{:S(2)}) async-start(s32[8,8,128]{2,1,0:T(8,128)} %shard_map.46), calls=%async_computation | async-start | bytes 65536 | tf_op jit(solution)/shard_map/all_to_all | solution.py:188
  27.3 22.9 %all-to-all-start.1 = ((bf16[8,4,16,256]{3,2,1,0:T(8,128)(2,1)}), bf16[8,4,16,256]{3,2,1,0:T(8,128)(2,1)S(1)}, u32[]{:S(2)}, u32[]{:S(2)}) async-start(bf16[8,4,16,256]{3,2,1,0:T(8,128)(2,1)} %shard_map.48), calls=%async_computation.1 | async-start | bytes 524288 | tf_op jit(solution)/shard_map/all_to_all | solution.py:188
  38.5 1.4 %copy-start.1 = (bf16[12,256,256]{2,1,0:T(8,128)(2,1)S(1)}, bf16[12,256,256]{2,1,0:T(8,128)(2,1)}, u32[]{:S(2)}) copy-start(bf16[12,256,256]{2,1,0:T(8,128)(2,1)} %tiles_ref.1) | copy-start | bytes 4718596
  78.9 17.2 %copy-start = (bf16[2048,768]{1,0:T(8,128)(2,1)S(1)}, bf16[2048,768]{1,0:T(8,128)(2,1)}, u32[]{:S(2)}) copy-start(bf16[2048,768]{1,0:T(8,128)(2,1)} %dosages_ref.1) | copy-start | bytes 9437188

commit v6 on v5

--- a/solution.py
+++ b/solution.py
@@ -9,7 +9,8 @@
 
 NEAR = 4
 LANES = 128
-TURN, VAR_TURN = 5, 15
+LIST_TURN, TRAIT_TURN, FIRST_TURN, VAR_TURN = 5, 4, 4, 15
+CHIP_TURN = 8
 NONE = -1
 VMEM = pl.BlockSpec(memory_space=pltpu.VMEM)
 HBM = pl.BlockSpec(memory_space=pltpu.HBM)
@@ -44,11 +45,13 @@
         out_ref[k] = listed
 
 
-def pack_kernel(here, block, lists_ref, near_ref, out_ref):
+def pack_kernel(here, block, turn, lists_ref, near_ref, out_ref):
     first = lax.axis_index("subj") // NEAR * (NEAR * here)
-    for k in range(out_ref.shape[0]):
+    far = out_ref.shape[0]
+    for k in range(far):
+        listed = place(k + turn, far, LIST_TURN)
         for j in range(out_ref.shape[1]):
-            inside = jnp.clip(lists_ref[k, 0, j] - first, 0, NEAR * here - 1)
+            inside = jnp.clip(lists_ref[listed, 0, j] - first, 0, NEAR * here - 1)
             at = pl.multiple_of(inside % here * block, block)
             out_ref[k, j] = near_ref[inside // here, :, pl.ds(at, block)]
 
@@ -60,7 +63,7 @@
 def apply_tiles(here, block, lists_ref, field_ref, other_ref, tiles_ref, sum_ref):
     me = lax.axis_index("subj")
     far, slots = other_ref.shape[:2]
-    mine = place(me // NEAR, far, TURN)
+    mine = place(me // NEAR, far, LIST_TURN)
     sum_ref[...] = jnp.zeros_like(sum_ref)
     count = jnp.int32(0)
     for t in range(tiles_ref.shape[0]):
@@ -69,7 +72,7 @@
         local = col // here == me
         at = pl.multiple_of(col % here * block, block)
         own = field_ref[:, pl.ds(at, block)]
-        other = other_ref[place(col // (here * NEAR), far, TURN), jnp.minimum(count, slots - 1)]
+        other = other_ref[place(col // (here * NEAR), far, FIRST_TURN), jnp.minimum(count, slots - 1)]
         count = count + jnp.where(local, 0, 1)
         slab = jnp.where(local, own, other)
         prod = tile_dot(slab, tiles_ref[t])
@@ -79,7 +82,7 @@
 
 def local_kernel(here, block, lists_ref, near_ref, tiles_ref, sum_ref, held_ref, sem):
     me = lax.axis_index("subj")
-    mine = place(me // NEAR, lists_ref.shape[0], TURN)
+    mine = place(me // NEAR, lists_ref.shape[0], LIST_TURN)
     copy = pltpu.make_async_copy(tiles_ref, held_ref, sem)
     copy.start()
     sum_ref[...] = jnp.zeros_like(sum_ref)
@@ -97,13 +100,13 @@
 def first_kernel(here, block, lists_ref, local_ref, other_ref, tiles_ref, sum_ref, sent_ref):
     me = lax.axis_index("subj")
     far = lists_ref.shape[0]
-    mine = place(me // NEAR, far, TURN)
+    mine = place(me // NEAR, far, LIST_TURN)
     sum_ref[...] = local_ref[...]
     for j in range(other_ref.shape[1]):
         col = lists_ref[mine, 0, j]
         t = jnp.maximum(lists_ref[mine, 3, j], 0)
         row = lists_ref[mine, 1, t] - me * here
-        slab = other_ref[place(jnp.maximum(col, 0) // (here * NEAR), far, TURN), j]
+        slab = other_ref[place(jnp.maximum(col, 0) // (here * NEAR), far, TRAIT_TURN), j]
         slab = jnp.where(col >= 0, slab, jnp.zeros_like(slab))
         to = pl.ds(pl.multiple_of(row * block, block), block)
         sum_ref[:, to] += tile_dot(slab, tiles_ref[t])
@@ -135,7 +138,7 @@
         for r in range(0, step, 8):
             owner, inner = divmod(i * step + r, rows)
             to = core if owner % 2 == 0 else 1 - core
-            out_ref[to, place(owner // 2, out_ref.shape[1], 2 * TURN), inner : inner + 8, :] = part[r : r + 8]
+            out_ref[to, place(owner // 2, out_ref.shape[1], CHIP_TURN), inner : inner + 8, :] = part[r : r + 8]
 
 
 def add_kernel(parts_ref, both_ref, out_ref):
@@ -177,31 +180,33 @@
     slots = tiles - here
     far = n // NEAR
     near_groups = [list(range(k, k + NEAR)) for k in range(0, n, NEAR)]
-    far_groups = [turned(list(range(i, n, NEAR)), TURN) for i in range(NEAR)]
-    chip_groups = [turned(list(range(c, n, 2)), 2 * TURN) for c in range(2)]
+    chip_groups = [turned(list(range(c, n, 2)), CHIP_TURN) for c in range(2)]
     var_groups = [turned(list(range(m)), VAR_TURN)]
     core_groups = [[s, s + 1] for s in range(0, n, 2)]
     f32, bf16 = jnp.float32, jnp.bfloat16
     sds = jax.ShapeDtypeStruct
 
+    def far_groups(turn):
+        return [turned(list(range(i, n, NEAR)), turn) for i in range(NEAR)]
+
     def exchanged(x, groups):
         return lax.all_to_all(x, "subj", 0, 0, tiled=True, axis_index_groups=groups)
 
     def gathered(field):
         return lax.all_gather(field, "subj", axis_index_groups=near_groups)
 
-    def fetched(lists, near):
+    def fetched(lists, near, turn):
         packed = call(
-            functools.partial(pack_kernel, here, block),
+            functools.partial(pack_kernel, here, block, turn),
             sds((far, slots, width, block), bf16),
             [SMEM, VMEM],
         )(lists, near)
-        return exchanged(packed, far_groups)
+        return exchanged(packed, far_groups(turn))
 
     lists = call(
         functools.partial(list_kernel, here), sds((far, 8, LANES), jnp.int32), [SMEM], mib=62
     )(kin_index.T)
-    lists = exchanged(lists, far_groups)[:, :4, :tiles]
+    lists = exchanged(lists, far_groups(LIST_TURN))[:, :4, :tiles]
     near = gathered(traits.T)
     local, held = call(
         functools.partial(local_kernel, here, block),
@@ -213,13 +218,13 @@
         functools.partial(first_kernel, here, block),
         [sds((width, rows_here), f32), sds((width, rows_here), bf16)],
         [SMEM, VMEM, VMEM, VMEM],
-    )(lists, local, fetched(lists, near), held)
+    )(lists, local, fetched(lists, near, TRAIT_TURN), held)
     copies = call(
         functools.partial(second_kernel, here, block),
         sds((m, width, rows_here), bf16),
         [SMEM, VMEM, VMEM, VMEM, VMEM, VMEM],
         [pltpu.VMEM((width, rows_here), f32)],
-    )(lists, sent, fetched(lists, gathered(sent)), held, first, near)
+    )(lists, sent, fetched(lists, gathered(sent), FIRST_TURN), held, first, near)
     wide = lax.all_to_all(copies, "var", 0, 0, tiled=True, axis_index_groups=var_groups)
     wide = wide.reshape(m * width, rows_here)
 

time: 133 us -> 132 us (level)
  blocking collectives: 84.3 us -> 82.5 us
    all_gather x1, blocking collectives: 9.87 us -> 4.21 us  [on_device(): both = lax.all_gather(parts[1], 'subj', axis_index_groups=core_groups)]
    all_to_all x1, blocking collectives: 15.8 us -> 19.9 us  [on_device(): lax.all_to_all(copies, 'var', 0, 0, tiled=True, axis_index_groups=var_gro...]
    all_gather x2, blocking collectives: 16.1 us -> 13.8 us  [gathered(): return lax.all_gather(field, 'subj', axis_index_groups=near_groups)]
    all_to_all x2, blocking collectives: 42.6 us -> 44.7 us  [exchanged(): return lax.all_to_all(x, 'subj', 0, 0, tiled=True, axis_index_groups=groups)]
where the time goes in v6:
time: 132 us
  blocking collectives  82.5 us (62%)
  starting transfers between devices  28.3 us (21%)
  Pallas kernels  9.91 us (8%)
  waiting for transfers between devices  9.45 us (7%)
  local copies, waits for them, and re-layouts  1.44 us (1%)
    all_to_all x2, blocking collectives, exchanged(): return lax.all_to_all(x, 'subj', 0, 0, tiled=True, axis_index_groups=groups)  44.7 us
    all_to_all x2, starting transfers between devices, exchanged(): return lax.all_to_all(x, 'subj', 0, 0, tiled=True, axis_index_groups=groups)  28.3 us
    all_to_all x1, blocking collectives, on_device(): lax.all_to_all(copies, 'var', 0, 0, tiled=True, axis_index_groups=var_gro...  19.9 us
    all_gather x2, blocking collectives, gathered(): return lax.all_gather(field, 'subj', axis_index_groups=near_groups)  13.8 us
    all_to_all x2, waiting for transfers between devices, exchanged(): return lax.all_to_all(x, 'subj', 0, 0, tiled=True, axis_index_groups=groups)  9.45 us
    all_gather x1, blocking collectives, on_device(): both = lax.all_gather(parts[1], 'subj', axis_index_groups=core_groups)  4.21 us
    pallas_call x2, Pallas kernels, fetched(): call(functools.partial(pack_kernel, here, block, turn), sds((far, slots,...  2.75 us
  transfers between devices with their start and end apart: 2, of which 1 were waited for; matrix products, arithmetic and copies ran while one was open for 0% of the time, Pallas kernels for 1%

profile of v6, /device:TPU:1, one launch (start us, length us, event | category | flops | bytes accessed | tf_op | source)
XLA Modules:
  0.0 131.7 jit_solution(14669388837001060173)
XLA Ops:
  0.0 1.4 %shard_map.46 = s32[8,8,128]{2,1,0:T(8,128)} custom-call(s32[2,12]{1,0:T(2,128)} %bitcast.11), custom_call_target="tpu_custom_call" | custom-call | tf_op jit(solution)/shard_map/pallas_call | solution.py:206
  1.4 16.9 %all-to-all-start = ((s32[8,8,128]{2,1,0:T(8,128)}), s32[8,8,128]{2,1,0:T(8,128)S(1)}, u32[]{:S(2)}, u32[]{:S(2)}) async-start(s32[8,8,128]{2,1,0:T(8,128)} %shard_map.46), calls=%async_computation | async-start | bytes 65536 | tf_op jit(solution)/shard_map/all_to_all | solution.py:193
  18.2 7.3 %all-gather = bf16[64,2048]{1,0:T(8,128)(2,1)S(1)} all-gather(bf16[16,2048]{1,0:T(8,128)(2,1)} %bitcast.10), channel_id=2, replica_groups={{0,16,32,48},{64,80,96,112},{128,144,160,176},{192,208,224,240},{256,27..., dimensions={0}, use_global_device_ids=true | all-gather | bytes 327680 | tf_op jit(solution)/shard_map/all_gather | solution.py:196
  25.5 0.0 all-to-all-done
  25.6 1.7 %shard_map.48 = bf16[8,4,16,256]{3,2,1,0:T(8,128)(2,1)} custom-call(s32[8,4,12]{2,1,0:T(4,128)S(1)} %slice.8.lists_ref, bf16[4,16,2048]{2,1,0:T(8,128)(2,1)S(1)} %bitcast.6), custom_call_target="tpu_custom_call" | custom-call | tf_op jit(solution)/shard_map/pallas_call | solution.py:199
  27.3 11.5 %all-to-all-start.1 = ((bf16[8,4,16,256]{3,2,1,0:T(8,128)(2,1)}), bf16[8,4,16,256]{3,2,1,0:T(8,128)(2,1)S(1)}, u32[]{:S(2)}, u32[]{:S(2)}) async-start(bf16[8,4,16,256]{3,2,1,0:T(8,128)(2,1)} %shard_map.48), calls=%async_computation.1 | async-start | bytes 524288 | tf_op jit(solution)/shard_map/all_to_all | solution.py:193
  38.7 0.0 copy-start.1
  38.7 1.4 %copy-done.1 = bf16[12,256,256]{2,1,0:T(8,128)(2,1)S(1)} copy-done((bf16[12,256,256]{2,1,0:T(8,128)(2,1)S(1)}, bf16[12,256,256]{2,1,0:T(8,128)(2,1)}, u32[]{:S(2)}) %copy-start.1) | copy-done | bytes 1572888
  40.1 1.5 %shard_map.47 = (f32[16,2048]{1,0:T(8,128)S(1)}, bf16[12,256,256]{2,1,0:T(8,128)(2,1)S(1)}) custom-call(s32[8,4,12]{2,1,0:T(4,128)S(1)} %slice.8.lists_ref, bf16[4,16,2048]{2,1,0:T(8,128)(2,1)S(1)} %bitcast.7, bf16[12,256,256]{2,1,0:T(8,128)(2,1)S(1)} %copy-done.1), custom_call_target="tpu_custom_call" | custom-call | tf_op jit(solution)/shard_map/pallas_call | solution.py:211
  41.6 9.4 %all-to-all-done.1.other_ref = bf16[8,4,16,256]{3,2,1,0:T(8,128)(2,1)S(1)} async-done(((bf16[8,4,16,256]{3,2,1,0:T(8,128)(2,1)}), bf16[8,4,16,256]{3,2,1,0:T(8,128)(2,1)S(1)}, u32[]{:S(2)}, u32[]{:S(2)}) %all-to-all-start.1) | async-done | bytes 262176 | tf_op jit(solution)/shard_map/all_to_all | solution.py:193
  51.1 1.1 shard_map.49
  52.2 6.5 %all-gather.1 = bf16[64,2048]{1,0:T(8,128)(2,1)S(1)} all-gather(bf16[16,2048]{1,0:T(8,128)(2,1)S(1)} %get-tuple-element.11.sent_ref), channel_id=3, replica_groups={{0,16,32,48},{64,80,96,112},{128,144,160,176},{192,208,224,240},{256,27..., dimensions={0}, use_global_device_ids=true | all-gather | bytes 327680 | tf_op jit(solution)/shard_map/all_gather | solution.py:196
  58.6 1.0 shard_map.50
  59.7 23.6 %all_to_all.25.other_ref = bf16[8,4,16,256]{3,2,1,0:T(8,128)(2,1)S(1)} all-to-all(bf16[8,4,16,256]{3,2,1,0:T(8,128)(2,1)S(1)} %shard_map.50), channel_id=1, replica_groups={{256,320,384,448,0,64,128,192},{272,336,400,464,16,80,144,208},{288,352..., dimensions={0} | all-to-all | bytes 524288 | tf_op jit(solution)/shard_map/all_to_all | solution.py:193
  83.3 0.0 copy-start
  83.3 1.4 %shard_map.51 = bf16[16,16,2048]{2,1,0:T(8,128)(2,1)S(1)} custom-call(s32[8,4,12]{2,1,0:T(4,128)S(1)} %slice.8.lists_ref, bf16[16,2048]{1,0:T(8,128)(2,1)S(1)} %get-tuple-element.11.sent_ref, bf16[8,4,16,256]{3,2,1,0:T(8,128)(2,1)S(1)} %all_to_all.25.other_ref, bf16[12,256,256]{2,1,0:T(8,128)(2,1)S(1)} %get-tuple-element.10.tiles_ref, ...), custom_call_target="tpu_custom_call" | custom-call | tf_op jit(solution)/shard_map/pallas_call | solution.py:222
  84.7 19.9 %all_to_all.26 = bf16[16,16,2048]{2,1,0:T(8,128)(2,1)S(1)} all-to-all(bf16[16,16,2048]{2,1,0:T(8,128)(2,1)S(1)} %shard_map.51), channel_id=1, replica_groups={{15,0,1,2,3,4,5,6,7,8,9,10,11,12,13,14},{31,16,17,18,19,20,21,22,23,24,..., dimensions={0} | all-to-all | bytes 2097152 | tf_op jit(solution)/shard_map/all_to_all | solution.py:228
  104.6 0.0 copy-done
  104.6 1.1 shard_map.52.parts_ref
  105.8 4.2 %all_gather.19.both_ref = f32[2,16,24,256]{3,2,1,0:T(8,128)S(1)} all-gather(f32[1,16,24,256]{3,2,1,0:T(8,128)S(1)} %slice.9), channel_id=1, replica_groups={{0,16},{32,48},{64,80},{96,112},{128,144},{160,176},{192,208},{224,240}..., dimensions={0}, use_global_device_ids=true | all-gather | bytes 1179648 | tf_op jit(solution)/shard_map/all_gather | solution.py:235
  110.0 21.0 %all_to_all.27.parts_ref = bf16[16,48,128]{2,1,0:T(8,128)(2,1)S(1)} all-to-all(bf16[16,48,128]{2,1,0:T(8,128)(2,1)S(1)} %shard_map.53), channel_id=1, replica_groups={{256,288,320,352,384,416,448,480,0,32,64,96,128,160,192,224},{272,304,3..., dimensions={0} | all-to-all | bytes 393216 | tf_op jit(solution)/shard_map/all_to_all | solution.py:193
  131.1 0.6 shard_map.54
  (3 shorter events, 0.1 us)
Async XLA Ops:
  1.4 24.2 %all-to-all-start = ((s32[8,8,128]{2,1,0:T(8,128)}), s32[8,8,128]{2,1,0:T(8,128)S(1)}, u32[]{:S(2)}, u32[]{:S(2)}) async-start(s32[8,8,128]{2,1,0:T(8,128)} %shard_map.46), calls=%async_computation | async-start | bytes 65536 | tf_op jit(solution)/shard_map/all_to_all | solution.py:193
  27.3 23.8 %all-to-all-start.1 = ((bf16[8,4,16,256]{3,2,1,0:T(8,128)(2,1)}), bf16[8,4,16,256]{3,2,1,0:T(8,128)(2,1)S(1)}, u32[]{:S(2)}, u32[]{:S(2)}) async-start(bf16[8,4,16,256]{3,2,1,0:T(8,128)(2,1)} %shard_map.48), calls=%async_computation.1 | async-start | bytes 524288 | tf_op jit(solution)/shard_map/all_to_all | solution.py:193
  38.7 1.4 %copy-start.1 = (bf16[12,256,256]{2,1,0:T(8,128)(2,1)S(1)}, bf16[12,256,256]{2,1,0:T(8,128)(2,1)}, u32[]{:S(2)}) copy-start(bf16[12,256,256]{2,1,0:T(8,128)(2,1)} %tiles_ref.1) | copy-start | bytes 4718596
  83.3 21.3 %copy-start = (bf16[2048,768]{1,0:T(8,128)(2,1)S(1)}, bf16[2048,768]{1,0:T(8,128)(2,1)}, u32[]{:S(2)}) copy-start(bf16[2048,768]{1,0:T(8,128)(2,1)} %dosages_ref.1) | copy-start | bytes 9437188

commit v7 on v6

--- a/solution.py
+++ b/solution.py
@@ -9,7 +9,7 @@
 
 NEAR = 4
 LANES = 128
-LIST_TURN, TRAIT_TURN, FIRST_TURN, VAR_TURN = 5, 4, 4, 15
+LIST_TURN, TRAIT_TURN, FIRST_TURN, VAR_TURN = 6, 4, 4, 15
 CHIP_TURN = 8
 NONE = -1
 VMEM = pl.BlockSpec(memory_space=pltpu.VMEM)

time: 132 us -> 131 us (level)
  waiting for transfers between devices: 9.45 us -> 7.06 us
  blocking collectives: 82.5 us -> 84.8 us
    all_to_all x2, waiting for transfers between devices: 9.45 us -> 7.06 us  [exchanged(): return lax.all_to_all(x, 'subj', 0, 0, tiled=True, axis_index_groups=groups)]
    all_gather x2, blocking collectives: 13.8 us -> 15.9 us  [gathered(): return lax.all_gather(field, 'subj', axis_index_groups=near_groups)]
where the time goes in v7:
time: 131 us
  blocking collectives  84.8 us (65%)
  starting transfers between devices  27.5 us (21%)
  Pallas kernels  9.91 us (8%)
  waiting for transfers between devices  7.06 us (5%)
  local copies, waits for them, and re-layouts  1.44 us (1%)
    all_to_all x2, blocking collectives, exchanged(): return lax.all_to_all(x, 'subj', 0, 0, tiled=True, axis_index_groups=groups)  44.9 us
    all_to_all x2, starting transfers between devices, exchanged(): return lax.all_to_all(x, 'subj', 0, 0, tiled=True, axis_index_groups=groups)  27.5 us
    all_to_all x1, blocking collectives, on_device(): lax.all_to_all(copies, 'var', 0, 0, tiled=True, axis_index_groups=var_gro...  19.8 us
    all_gather x2, blocking collectives, gathered(): return lax.all_gather(field, 'subj', axis_index_groups=near_groups)  15.9 us
    all_to_all x2, waiting for transfers between devices, exchanged(): return lax.all_to_all(x, 'subj', 0, 0, tiled=True, axis_index_groups=groups)  7.06 us
    all_gather x1, blocking collectives, on_device(): both = lax.all_gather(parts[1], 'subj', axis_index_groups=core_groups)  4.29 us
    pallas_call x2, Pallas kernels, fetched(): call(functools.partial(pack_kernel, here, block, turn), sds((far, slots,...  2.75 us
  transfers between devices with their start and end apart: 2, of which 1 were waited for; matrix products, arithmetic and copies ran while one was open for 0% of the time, Pallas kernels for 1%

profile of v7, /device:TPU:1, one launch (start us, length us, event | category | flops | bytes accessed | tf_op | source)
XLA Modules:
  0.0 130.8 jit_solution(9857056412324816863)
XLA Ops:
  0.0 1.4 %shard_map.46 = s32[8,8,128]{2,1,0:T(8,128)} custom-call(s32[2,12]{1,0:T(2,128)} %bitcast.11), custom_call_target="tpu_custom_call" | custom-call | tf_op jit(solution)/shard_map/pallas_call | solution.py:206
  1.4 15.9 %all-to-all-start = ((s32[8,8,128]{2,1,0:T(8,128)}), s32[8,8,128]{2,1,0:T(8,128)S(1)}, u32[]{:S(2)}, u32[]{:S(2)}) async-start(s32[8,8,128]{2,1,0:T(8,128)} %shard_map.46), calls=%async_computation | async-start | bytes 65536 | tf_op jit(solution)/shard_map/all_to_all | solution.py:193
  17.3 7.2 %all-gather = bf16[64,2048]{1,0:T(8,128)(2,1)S(1)} all-gather(bf16[16,2048]{1,0:T(8,128)(2,1)} %bitcast.10), channel_id=2, replica_groups={{0,16,32,48},{64,80,96,112},{128,144,160,176},{192,208,224,240},{256,27..., dimensions={0}, use_global_device_ids=true | all-gather | bytes 327680 | tf_op jit(solution)/shard_map/all_gather | solution.py:196
  24.5 0.0 all-to-all-done
  24.5 1.7 %shard_map.48 = bf16[8,4,16,256]{3,2,1,0:T(8,128)(2,1)} custom-call(s32[8,4,12]{2,1,0:T(4,128)S(1)} %slice.8.lists_ref, bf16[4,16,2048]{2,1,0:T(8,128)(2,1)S(1)} %bitcast.6), custom_call_target="tpu_custom_call" | custom-call | tf_op jit(solution)/shard_map/pallas_call | solution.py:199
  26.2 11.6 %all-to-all-start.1 = ((bf16[8,4,16,256]{3,2,1,0:T(8,128)(2,1)}), bf16[8,4,16,256]{3,2,1,0:T(8,128)(2,1)S(1)}, u32[]{:S(2)}, u32[]{:S(2)}) async-start(bf16[8,4,16,256]{3,2,1,0:T(8,128)(2,1)} %shard_map.48), calls=%async_computation.1 | async-start | bytes 524288 | tf_op jit(solution)/shard_map/all_to_all | solution.py:193
  37.8 0.0 copy-start.1
  37.8 1.4 %copy-done.1 = bf16[12,256,256]{2,1,0:T(8,128)(2,1)S(1)} copy-done((bf16[12,256,256]{2,1,0:T(8,128)(2,1)S(1)}, bf16[12,256,256]{2,1,0:T(8,128)(2,1)}, u32[]{:S(2)}) %copy-start.1) | copy-done | bytes 1572888
  39.2 1.5 %shard_map.47 = (f32[16,2048]{1,0:T(8,128)S(1)}, bf16[12,256,256]{2,1,0:T(8,128)(2,1)S(1)}) custom-call(s32[8,4,12]{2,1,0:T(4,128)S(1)} %slice.8.lists_ref, bf16[4,16,2048]{2,1,0:T(8,128)(2,1)S(1)} %bitcast.7, bf16[12,256,256]{2,1,0:T(8,128)(2,1)S(1)} %copy-done.1), custom_call_target="tpu_custom_call" | custom-call | tf_op jit(solution)/shard_map/pallas_call | solution.py:211
  40.7 7.1 %all-to-all-done.1.other_ref = bf16[8,4,16,256]{3,2,1,0:T(8,128)(2,1)S(1)} async-done(((bf16[8,4,16,256]{3,2,1,0:T(8,128)(2,1)}), bf16[8,4,16,256]{3,2,1,0:T(8,128)(2,1)S(1)}, u32[]{:S(2)}, u32[]{:S(2)}) %all-to-all-start.1) | async-done | bytes 262176 | tf_op jit(solution)/shard_map/all_to_all | solution.py:193
  47.7 1.1 shard_map.49
  48.8 8.7 %all-gather.1 = bf16[64,2048]{1,0:T(8,128)(2,1)S(1)} all-gather(bf16[16,2048]{1,0:T(8,128)(2,1)S(1)} %get-tuple-element.11.sent_ref), channel_id=3, replica_groups={{0,16,32,48},{64,80,96,112},{128,144,160,176},{192,208,224,240},{256,27..., dimensions={0}, use_global_device_ids=true | all-gather | bytes 327680 | tf_op jit(solution)/shard_map/all_gather | solution.py:196
  57.5 1.0 shard_map.50
  58.6 23.8 %all_to_all.25.other_ref = bf16[8,4,16,256]{3,2,1,0:T(8,128)(2,1)S(1)} all-to-all(bf16[8,4,16,256]{3,2,1,0:T(8,128)(2,1)S(1)} %shard_map.50), channel_id=1, replica_groups={{256,320,384,448,0,64,128,192},{272,336,400,464,16,80,144,208},{288,352..., dimensions={0} | all-to-all | bytes 524288 | tf_op jit(solution)/shard_map/all_to_all | solution.py:193
  82.4 0.0 copy-start
  82.4 1.4 %shard_map.51 = bf16[16,16,2048]{2,1,0:T(8,128)(2,1)S(1)} custom-call(s32[8,4,12]{2,1,0:T(4,128)S(1)} %slice.8.lists_ref, bf16[16,2048]{1,0:T(8,128)(2,1)S(1)} %get-tuple-element.11.sent_ref, bf16[8,4,16,256]{3,2,1,0:T(8,128)(2,1)S(1)} %all_to_all.25.other_ref, bf16[12,256,256]{2,1,0:T(8,128)(2,1)S(1)} %get-tuple-element.10.tiles_ref, ...), custom_call_target="tpu_custom_call" | custom-call | tf_op jit(solution)/shard_map/pallas_call | solution.py:222
  83.8 19.8 %all_to_all.26 = bf16[16,16,2048]{2,1,0:T(8,128)(2,1)S(1)} all-to-all(bf16[16,16,2048]{2,1,0:T(8,128)(2,1)S(1)} %shard_map.51), channel_id=1, replica_groups={{15,0,1,2,3,4,5,6,7,8,9,10,11,12,13,14},{31,16,17,18,19,20,21,22,23,24,..., dimensions={0} | all-to-all | bytes 2097152 | tf_op jit(solution)/shard_map/all_to_all | solution.py:228
  103.6 0.0 copy-done
  103.6 1.1 shard_map.52.parts_ref
  104.8 4.3 %all_gather.19.both_ref = f32[2,16,24,256]{3,2,1,0:T(8,128)S(1)} all-gather(f32[1,16,24,256]{3,2,1,0:T(8,128)S(1)} %slice.9), channel_id=1, replica_groups={{0,16},{32,48},{64,80},{96,112},{128,144},{160,176},{192,208},{224,240}..., dimensions={0}, use_global_device_ids=true | all-gather | bytes 1179648 | tf_op jit(solution)/shard_map/all_gather | solution.py:235
  109.1 21.0 %all_to_all.27.parts_ref = bf16[16,48,128]{2,1,0:T(8,128)(2,1)S(1)} all-to-all(bf16[16,48,128]{2,1,0:T(8,128)(2,1)S(1)} %shard_map.53), channel_id=1, replica_groups={{256,288,320,352,384,416,448,480,0,32,64,96,128,160,192,224},{272,304,3..., dimensions={0} | all-to-all | bytes 393216 | tf_op jit(solution)/shard_map/all_to_all | solution.py:193
  130.2 0.6 shard_map.54
  (3 shorter events, 0.1 us)
Async XLA Ops:
  1.4 23.1 %all-to-all-start = ((s32[8,8,128]{2,1,0:T(8,128)}), s32[8,8,128]{2,1,0:T(8,128)S(1)}, u32[]{:S(2)}, u32[]{:S(2)}) async-start(s32[8,8,128]{2,1,0:T(8,128)} %shard_map.46), calls=%async_computation | async-start | bytes 65536 | tf_op jit(solution)/shard_map/all_to_all | solution.py:193
  26.2 21.5 %all-to-all-start.1 = ((bf16[8,4,16,256]{3,2,1,0:T(8,128)(2,1)}), bf16[8,4,16,256]{3,2,1,0:T(8,128)(2,1)S(1)}, u32[]{:S(2)}, u32[]{:S(2)}) async-start(bf16[8,4,16,256]{3,2,1,0:T(8,128)(2,1)} %shard_map.48), calls=%async_computation.1 | async-start | bytes 524288 | tf_op jit(solution)/shard_map/all_to_all | solution.py:193
  37.8 1.4 %copy-start.1 = (bf16[12,256,256]{2,1,0:T(8,128)(2,1)S(1)}, bf16[12,256,256]{2,1,0:T(8,128)(2,1)}, u32[]{:S(2)}) copy-start(bf16[12,256,256]{2,1,0:T(8,128)(2,1)} %tiles_ref.1) | copy-start | bytes 4718596
  82.4 21.2 %copy-start = (bf16[2048,768]{1,0:T(8,128)(2,1)S(1)}, bf16[2048,768]{1,0:T(8,128)(2,1)}, u32[]{:S(2)}) copy-start(bf16[2048,768]{1,0:T(8,128)(2,1)} %dosages_ref.1) | copy-start | bytes 9437188

commit v8 on v7

--- a/solution.py
+++ b/solution.py
@@ -143,11 +143,10 @@
 
 def add_kernel(parts_ref, both_ref, out_ref):
     other = 1 - lax.axis_index("subj") % 2
-    rows, lanes = parts_ref.shape[2], out_ref.shape[2]
-    for i in range(out_ref.shape[1] // rows):
-        part = slice(i * lanes, (i + 1) * lanes)
-        total = parts_ref[0, :, :, part] + both_ref[other, :, :, part]
-        out_ref[:, i * rows : (i + 1) * rows, :] = total.astype(out_ref.dtype)
+    lanes = out_ref.shape[2]
+    total = parts_ref[0] + both_ref[other]
+    halves = [total[:, :, i : i + lanes] for i in range(0, total.shape[2], lanes)]
+    out_ref[...] = jnp.concatenate(halves, axis=1).astype(out_ref.dtype)
 
 
 def sum_kernel(parts_ref, out_ref):

time: 131 us -> 131 us (level)
  no operation moved by 1% of the time
where the time goes in v8:
time: 131 us
  blocking collectives  84.8 us (65%)
  starting transfers between devices  27.5 us (21%)
  Pallas kernels  9.9 us (8%)
  waiting for transfers between devices  7.06 us (5%)
  local copies, waits for them, and re-layouts  1.44 us (1%)
    all_to_all x2, blocking collectives, exchanged(): return lax.all_to_all(x, 'subj', 0, 0, tiled=True, axis_index_groups=groups)  44.9 us
    all_to_all x2, starting transfers between devices, exchanged(): return lax.all_to_all(x, 'subj', 0, 0, tiled=True, axis_index_groups=groups)  27.5 us
    all_to_all x1, blocking collectives, on_device(): lax.all_to_all(copies, 'var', 0, 0, tiled=True, axis_index_groups=var_gro...  19.8 us
    all_gather x2, blocking collectives, gathered(): return lax.all_gather(field, 'subj', axis_index_groups=near_groups)  15.9 us
    all_to_all x2, waiting for transfers between devices, exchanged(): return lax.all_to_all(x, 'subj', 0, 0, tiled=True, axis_index_groups=groups)  7.06 us
    all_gather x1, blocking collectives, on_device(): both = lax.all_gather(parts[1], 'subj', axis_index_groups=core_groups)  4.29 us
    pallas_call x2, Pallas kernels, fetched(): call(functools.partial(pack_kernel, here, block, turn), sds((far, slots,...  2.75 us
  transfers between devices with their start and end apart: 2, of which 1 were waited for; matrix products, arithmetic and copies ran while one was open for 0% of the time, Pallas kernels for 1%

profile of v8, /device:TPU:1, one launch (start us, length us, event | category | flops | bytes accessed | tf_op | source)
XLA Modules:
  0.0 130.8 jit_solution(3527085596907270050)
XLA Ops:
  0.0 1.4 %shard_map.46 = s32[8,8,128]{2,1,0:T(8,128)} custom-call(s32[2,12]{1,0:T(2,128)} %bitcast.11), custom_call_target="tpu_custom_call" | custom-call | tf_op jit(solution)/shard_map/pallas_call | solution.py:205
  1.4 15.9 %all-to-all-start = ((s32[8,8,128]{2,1,0:T(8,128)}), s32[8,8,128]{2,1,0:T(8,128)S(1)}, u32[]{:S(2)}, u32[]{:S(2)}) async-start(s32[8,8,128]{2,1,0:T(8,128)} %shard_map.46), calls=%async_computation | async-start | bytes 65536 | tf_op jit(solution)/shard_map/all_to_all | solution.py:192
  17.3 7.2 %all-gather = bf16[64,2048]{1,0:T(8,128)(2,1)S(1)} all-gather(bf16[16,2048]{1,0:T(8,128)(2,1)} %bitcast.10), channel_id=2, replica_groups={{0,16,32,48},{64,80,96,112},{128,144,160,176},{192,208,224,240},{256,27..., dimensions={0}, use_global_device_ids=true | all-gather | bytes 327680 | tf_op jit(solution)/shard_map/all_gather | solution.py:195
  24.5 0.0 all-to-all-done
  24.5 1.7 %shard_map.48 = bf16[8,4,16,256]{3,2,1,0:T(8,128)(2,1)} custom-call(s32[8,4,12]{2,1,0:T(4,128)S(1)} %slice.8.lists_ref, bf16[4,16,2048]{2,1,0:T(8,128)(2,1)S(1)} %bitcast.6), custom_call_target="tpu_custom_call" | custom-call | tf_op jit(solution)/shard_map/pallas_call | solution.py:198
  26.2 11.6 %all-to-all-start.1 = ((bf16[8,4,16,256]{3,2,1,0:T(8,128)(2,1)}), bf16[8,4,16,256]{3,2,1,0:T(8,128)(2,1)S(1)}, u32[]{:S(2)}, u32[]{:S(2)}) async-start(bf16[8,4,16,256]{3,2,1,0:T(8,128)(2,1)} %shard_map.48), calls=%async_computation.1 | async-start | bytes 524288 | tf_op jit(solution)/shard_map/all_to_all | solution.py:192
  37.8 0.0 copy-start.1
  37.8 1.4 %copy-done.1 = bf16[12,256,256]{2,1,0:T(8,128)(2,1)S(1)} copy-done((bf16[12,256,256]{2,1,0:T(8,128)(2,1)S(1)}, bf16[12,256,256]{2,1,0:T(8,128)(2,1)}, u32[]{:S(2)}) %copy-start.1) | copy-done | bytes 1572888
  39.2 1.5 %shard_map.47 = (f32[16,2048]{1,0:T(8,128)S(1)}, bf16[12,256,256]{2,1,0:T(8,128)(2,1)S(1)}) custom-call(s32[8,4,12]{2,1,0:T(4,128)S(1)} %slice.8.lists_ref, bf16[4,16,2048]{2,1,0:T(8,128)(2,1)S(1)} %bitcast.7, bf16[12,256,256]{2,1,0:T(8,128)(2,1)S(1)} %copy-done.1), custom_call_target="tpu_custom_call" | custom-call | tf_op jit(solution)/shard_map/pallas_call | solution.py:210
  40.7 7.1 %all-to-all-done.1.other_ref = bf16[8,4,16,256]{3,2,1,0:T(8,128)(2,1)S(1)} async-done(((bf16[8,4,16,256]{3,2,1,0:T(8,128)(2,1)}), bf16[8,4,16,256]{3,2,1,0:T(8,128)(2,1)S(1)}, u32[]{:S(2)}, u32[]{:S(2)}) %all-to-all-start.1) | async-done | bytes 262176 | tf_op jit(solution)/shard_map/all_to_all | solution.py:192
  47.7 1.1 shard_map.49
  48.8 8.7 %all-gather.1 = bf16[64,2048]{1,0:T(8,128)(2,1)S(1)} all-gather(bf16[16,2048]{1,0:T(8,128)(2,1)S(1)} %get-tuple-element.11.sent_ref), channel_id=3, replica_groups={{0,16,32,48},{64,80,96,112},{128,144,160,176},{192,208,224,240},{256,27..., dimensions={0}, use_global_device_ids=true | all-gather | bytes 327680 | tf_op jit(solution)/shard_map/all_gather | solution.py:195
  57.5 1.0 shard_map.50
  58.6 23.8 %all_to_all.25.other_ref = bf16[8,4,16,256]{3,2,1,0:T(8,128)(2,1)S(1)} all-to-all(bf16[8,4,16,256]{3,2,1,0:T(8,128)(2,1)S(1)} %shard_map.50), channel_id=1, replica_groups={{256,320,384,448,0,64,128,192},{272,336,400,464,16,80,144,208},{288,352..., dimensions={0} | all-to-all | bytes 524288 | tf_op jit(solution)/shard_map/all_to_all | solution.py:192
  82.4 0.0 copy-start
  82.4 1.4 %shard_map.51 = bf16[16,16,2048]{2,1,0:T(8,128)(2,1)S(1)} custom-call(s32[8,4,12]{2,1,0:T(4,128)S(1)} %slice.8.lists_ref, bf16[16,2048]{1,0:T(8,128)(2,1)S(1)} %get-tuple-element.11.sent_ref, bf16[8,4,16,256]{3,2,1,0:T(8,128)(2,1)S(1)} %all_to_all.25.other_ref, bf16[12,256,256]{2,1,0:T(8,128)(2,1)S(1)} %get-tuple-element.10.tiles_ref, ...), custom_call_target="tpu_custom_call" | custom-call | tf_op jit(solution)/shard_map/pallas_call | solution.py:221
  83.8 19.8 %all_to_all.26 = bf16[16,16,2048]{2,1,0:T(8,128)(2,1)S(1)} all-to-all(bf16[16,16,2048]{2,1,0:T(8,128)(2,1)S(1)} %shard_map.51), channel_id=1, replica_groups={{15,0,1,2,3,4,5,6,7,8,9,10,11,12,13,14},{31,16,17,18,19,20,21,22,23,24,..., dimensions={0} | all-to-all | bytes 2097152 | tf_op jit(solution)/shard_map/all_to_all | solution.py:227
  103.6 0.0 copy-done
  103.6 1.1 shard_map.52.parts_ref
  104.8 4.3 %all_gather.19.both_ref = f32[2,16,24,256]{3,2,1,0:T(8,128)S(1)} all-gather(f32[1,16,24,256]{3,2,1,0:T(8,128)S(1)} %slice.9), channel_id=1, replica_groups={{0,16},{32,48},{64,80},{96,112},{128,144},{160,176},{192,208},{224,240}..., dimensions={0}, use_global_device_ids=true | all-gather | bytes 1179648 | tf_op jit(solution)/shard_map/all_gather | solution.py:234
  109.1 21.0 %all_to_all.27.parts_ref = bf16[16,48,128]{2,1,0:T(8,128)(2,1)S(1)} all-to-all(bf16[16,48,128]{2,1,0:T(8,128)(2,1)S(1)} %shard_map.53), channel_id=1, replica_groups={{256,288,320,352,384,416,448,480,0,32,64,96,128,160,192,224},{272,304,3..., dimensions={0} | all-to-all | bytes 393216 | tf_op jit(solution)/shard_map/all_to_all | solution.py:192
  130.2 0.6 shard_map.54
  (3 shorter events, 0.1 us)
Async XLA Ops:
  1.4 23.1 %all-to-all-start = ((s32[8,8,128]{2,1,0:T(8,128)}), s32[8,8,128]{2,1,0:T(8,128)S(1)}, u32[]{:S(2)}, u32[]{:S(2)}) async-start(s32[8,8,128]{2,1,0:T(8,128)} %shard_map.46), calls=%async_computation | async-start | bytes 65536 | tf_op jit(solution)/shard_map/all_to_all | solution.py:192
  26.2 21.5 %all-to-all-start.1 = ((bf16[8,4,16,256]{3,2,1,0:T(8,128)(2,1)}), bf16[8,4,16,256]{3,2,1,0:T(8,128)(2,1)S(1)}, u32[]{:S(2)}, u32[]{:S(2)}) async-start(bf16[8,4,16,256]{3,2,1,0:T(8,128)(2,1)} %shard_map.48), calls=%async_computation.1 | async-start | bytes 524288 | tf_op jit(solution)/shard_map/all_to_all | solution.py:192
  37.8 1.4 %copy-start.1 = (bf16[12,256,256]{2,1,0:T(8,128)(2,1)S(1)}, bf16[12,256,256]{2,1,0:T(8,128)(2,1)}, u32[]{:S(2)}) copy-start(bf16[12,256,256]{2,1,0:T(8,128)(2,1)} %tiles_ref.1) | copy-start | bytes 4718596
  82.4 21.2 %copy-start = (bf16[2048,768]{1,0:T(8,128)(2,1)S(1)}, bf16[2048,768]{1,0:T(8,128)(2,1)}, u32[]{:S(2)}) copy-start(bf16[2048,768]{1,0:T(8,128)(2,1)} %dosages_ref.1) | copy-start | bytes 9437188
